TPU v7x, 32 devices: a whole 2x2x4 slice. The times are simulated.
32 devices in a mesh: dom: 8 (over y, x, core), rot: 4 (over z).
Axes of the slice: x: 2, y: 2, z: 4, core: 2. Of those that a mesh axis runs over, the one named last changes fastest.
Arguments:
- particles: bfloat16 [512, 8192], P('dom'), may hold values from -8 to 8, as said below
- assign: int32 [512], P('dom'), may hold values from 0 to 47, as said below
- rot_index: int32 [512], P('dom'), may hold values from 0 to 31
- group: int32 [512], P('dom'), may hold values from 0 to 31
- ctf_table: float32 [32, 64], replicated, may hold values from -1 to 1
Outputs:
- refs: bfloat16 [48, 8192], P('dom')
- best_scores: float32 [512, 48], P(('dom', 'rot'))
Inputs may be any that keep to these rules, and one draw needn't show every extreme that they name: `particles`: rows in custom order; values real. `assign`: owner o holds classes o * 6 to o * 6 + 5. The 64 particles of one index of dom form 4 shares of 16 consecutive particles; within each share at most 4 particles are assigned to the classes of one owner.
All inputs are finite; a program needn't handle non-finite values.
Results may differ from a plain program's by a relative error of at most 0.0027.
Values may be sent and summed in bfloat16 or wider, within the bound.
A program may use at most 128 MiB of HBM per device.

v0:
```python
import math

import jax
import jax.numpy as jnp
from jax import lax
from jax.sharding import PartitionSpec as P

CYCLES = 64
MFREQ = 64
CLS_DEV = 6
ROT_DEV = 8
K = 8192


def angles(index, total):
    freqs = jnp.arange(MFREQ, dtype=jnp.int32)
    phase = freqs[None, :] * index[:, None] % total
    return phase.astype(jnp.float32) * (2.0 * math.pi / total)


def derotate(spec, rotation, ctf_rows, total):
    count = spec.shape[0]
    layered = spec.reshape(count, 2, CYCLES, MFREQ)
    real_part = layered[:, 0]
    imag_part = layered[:, 1]
    angle = angles(rotation, total)
    cosine = jnp.cos(angle)[:, None, :]
    sine = jnp.sin(angle)[:, None, :]
    turned = jnp.stack(
        [real_part * cosine + imag_part * sine, imag_part * cosine - real_part * sine], axis=1
    )
    return (turned * ctf_rows[:, None, :, None]).reshape(count, K)


def rotate_refs(refs, rotation, total):
    count = refs.shape[0]
    layered = refs.astype(jnp.float32).reshape(count, 2, CYCLES, MFREQ)
    real_part = layered[:, 0]
    imag_part = layered[:, 1]
    angle = angles(jnp.reshape(rotation, (1,)), total)
    cosine = jnp.cos(angle)
    sine = jnp.sin(angle)
    turned = jnp.stack(
        [real_part * cosine - imag_part * sine, real_part * sine + imag_part * cosine], axis=1
    )
    return turned.reshape(count, K).astype(jnp.bfloat16)


def table_rows(group, ctf_table):
    onehot = (group[:, None] == jnp.arange(ctf_table.shape[0], dtype=jnp.int32)[None, :]).astype(
        jnp.float32
    )
    return jnp.dot(
        onehot, ctf_table, precision=lax.Precision.HIGHEST, preferred_element_type=jnp.float32
    )


def accumulate(spec, labels, rotation, group, ctf_table, count, total):
    ctf_rows = table_rows(group, ctf_table)
    weighted = derotate(spec.astype(jnp.float32), rotation, ctf_rows, total)
    member = (jnp.arange(count, dtype=jnp.int32)[:, None] == labels[None, :]).astype(jnp.float32)
    numer = jnp.dot(
        member, weighted, precision=lax.Precision.HIGHEST, preferred_element_type=jnp.float32
    )
    denom = jnp.dot(
        member,
        ctf_rows * ctf_rows,
        precision=lax.Precision.HIGHEST,
        preferred_element_type=jnp.float32,
    )
    return (numer, denom)


def local(particles, assign, rot_index, group, ctf_table):
    dom_count = lax.axis_size("dom")
    rot_count = lax.axis_size("rot")
    rot_rank = lax.axis_index("rot")
    total = ROT_DEV * rot_count
    share = particles.shape[0] // rot_count
    first = rot_rank * share
    mine = lax.dynamic_slice_in_dim(particles, first, share, 0)
    mine_assign = lax.dynamic_slice_in_dim(assign, first, share, 0)
    mine_rot = lax.dynamic_slice_in_dim(rot_index, first, share, 0)
    mine_group = lax.dynamic_slice_in_dim(group, first, share, 0)
    numer_all, denom_all = accumulate(
        mine, mine_assign, mine_rot, mine_group, ctf_table, CLS_DEV * dom_count, total
    )
    numer, denom = (
        lax.psum_scatter(numer_all, "dom", scatter_dimension=0, tiled=True),
        lax.psum_scatter(denom_all, "dom", scatter_dimension=0, tiled=True),
    )
    numer, denom = lax.psum((numer, denom), "rot")
    plain = numer.reshape(CLS_DEV, 2, CYCLES, MFREQ) / (denom[:, None, :, None] + 1.0)
    spread = jnp.mean(plain * plain, axis=(1, 2, 3))
    refs = (
        (plain / jnp.sqrt(spread + 1e-06)[:, None, None, None])
        .reshape(CLS_DEV, K)
        .astype(jnp.bfloat16)
    )
    ctf_all = table_rows(group, ctf_table)
    modulated = (
        (particles.reshape(-1, 2, CYCLES, MFREQ) * ctf_all[:, None, :, None])
        .reshape(-1, K)
        .astype(jnp.bfloat16)
    )
    scale = 1.0 / math.sqrt(K)
    piece = lax.all_gather(refs, "dom", axis=0, tiled=True)
    best = None
    for turn in range(ROT_DEV):
        rotation = rot_rank * ROT_DEV + turn
        turned = rotate_refs(piece, rotation, total)
        found = (
            lax.dot_general(
                modulated, turned, (((1,), (1,)), ((), ())), preferred_element_type=jnp.float32
            )
            * scale
        )
        best = found if best is None else jnp.maximum(best, found)
    highest = lax.pmax(best, "rot")
    best_scores = lax.dynamic_slice_in_dim(highest, first, share, 0)
    return (refs, best_scores)


def solution(mesh):
    in_specs = (P("dom", None), P("dom"), P("dom"), P("dom"), P())
    out_specs = (P("dom", None), P(("dom", "rot"), None))
    return jax.shard_map(local, mesh=mesh, in_specs=in_specs, out_specs=out_specs, check_vma=False)
```

profile of v0, /device:TPU:0, one launch (start us, length us, event | category | flops | bytes accessed | tf_op | source)
XLA Modules:
  0.0 216.5 jit_solution(4728262702142896131)
XLA Ops:
  7.3 1.0 dynamic-slice_convert_fusion
  10.1 0.8 fusion.10
  10.9 28.5 %fusion = f32[8,8192]{1,0:T(8,128)S(1)} fusion(f32[48,8192]{1,0:T(8,128)S(1)} %fusion.10), kind=kCustom, calls=%all-reduce-scatter | all-reduce-scatter fusion | flops 524289 | bytes 1835520
  39.4 2.0 collective-permute-start
  41.4 0.7 slice.16
  42.2 2.5 %collective-permute-start.1 = (f32[6,8192]{1,0:T(8,128)}, f32[6,8192]{1,0:T(8,128)}, u32[]{:S(2)}, u32[]{:S(2)}) collective-permute-start(f32[6,8192]{1,0:T(8,128)} %slice.16), channel_id=1, source_target_pairs={{0,8},{4,12},{8,16},{12,20},{16,24},{20,28},{1,9},{5,13},{9,17},{1... | collective-permute-start | bytes 589832
  45.0 24.9 %all-reduce.1 = f32[48,64]{1,0:T(8,128)S(1)} all-reduce(f32[48,64]{1,0:T(8,128)S(1)} %fusion.9), channel_id=3, replica_groups=mesh['dom'=8,'rot'=4] {'dom'}, use_global_device_ids=true, to_apply=%region_2.3.clone | all-reduce | flops 3072 | bytes 24576
  69.9 0.6 fusion.65
  71.2 12.0 %psum.15 = f32[6,64]{1,0:T(8,128)S(1)} all-reduce(f32[6,64]{1,0:T(8,128)S(1)} %constant_dynamic-slice_fusion.1), channel_id=1, replica_groups=mesh['dom'=8,'rot'=4] {'rot'}, use_global_device_ids=true, to_apply=%region_3.4 | all-reduce | flops 384 | bytes 3072 | tf_op jit(solution)/shard_map/psum | solution.py:92
  83.1 2.5 %mul.653 = f32[64,2,64,64]{3,2,1,0:T(8,128)} broadcast(f32[64,64]{1,0:T(8,128)S(1)} %fusion.8), dimensions={0,2} | broadcast | bytes 2113536 | tf_op jit(solution)/shard_map/mul | solution.py:102
  85.7 3.5 %mul.654 = f32[64,8192]{1,0:T(8,128)S(1)} reshape(f32[64,2,64,64]{3,2,1,0:T(8,128)} %mul.653) | data formatting | bytes 4194304 | tf_op jit(solution)/shard_map/mul | solution.py:102
  89.2 1.4 multiply_convert_fusion
  90.7 0.6 fusion.49
  91.4 0.6 fusion.61
  92.9 0.6 fusion.59
  93.5 0.6 fusion.51
  94.1 3.4 %concatenate = f32[22,8192]{1,0:T(8,128)S(1)} concatenate(f32[6,8192]{1,0:T(8,128)} %collective-permute-done.1, f32[8,8192]{1,0:T(8,128)} %collective-permute-done, f32[8,8192]{1,0:T(8,128)S(1)} %fusion), dimensions={0} | concatenate | bytes 1441792
  97.5 0.7 constant_dynamic-slice_fusion
  98.3 0.6 fusion.57
  98.9 0.6 fusion.55
  99.5 32.1 %all-reduce.5.cloned.1.call-done = f32[6,8192]{1,0:T(8,128)} async-done(((f32[6,8192]{1,0:T(8,128)}), f32[6,8192]{1,0:T(8,128)}) %all-reduce.5.cloned.1.call-update) | async-done | bytes 196624 | tf_op jit(solution)/shard_map/psum | solution.py:92
  131.6 1.1 multiply_reduce_fusion
  132.7 1.1 divide_convert_fusion
  133.8 10.9 %all-gather = bf16[8,6,8192]{2,1,0:T(8,128)(2,1)S(1)} all-gather(bf16[1,6,8192]{2,1,0:T(8,128)(2,1)S(1)} %bitcast.45), channel_id=1, replica_groups=mesh['dom'=8,'rot'=4] {'dom'}, dimensions={0}, use_global_device_ids=true | all-gather | bytes 884736 | tf_op jit(solution)/shard_map/all_gather | solution.py:107
  144.7 2.5 %reshape.402 = f32[48,2,64,64]{3,2,1,0:T(8,128)} reshape(bf16[8,6,8192]{2,1,0:T(8,128)(2,1)S(1)} %all-gather) | data formatting | bytes 2359296 | tf_op jit(solution)/shard_map/reshape | solution.py:37
  147.2 3.9 %subtract_convert_fusion.2 = (bf16[48,1,64,64]{3,2,1,0:T(8,128)(2,1)}, bf16[48,1,64,64]{3,2,1,0:T(8,128)(2,1)}, bf16[48,1,64,64]{3,2,1,0:T(8,128)(2,1)S(1)}, bf16[48,1,64,64]{3,2,1,0:T(8,128)(2,1)S(1)}) fusion(f32[64]{0:T(128)S(1)} %get-tuple-element.38, f32[64]{0:T(128)S(1)} %get-tuple-element.39, f32[48,2,64,64]{3,2,1,0:T(8,128)} %reshape.402, ...), kind=kLoop, calls=%fused_computation.14 | loop fusion | flops 3145728 | bytes 3146752 | tf_op jit(solution)/shard_map/convert.6
  151.4 1.3 convert_element_type.173
  152.8 4.8 %subtract_convert_fusion = (bf16[48,1,64,64]{3,2,1,0:T(8,128)(2,1)}, bf16[48,1,64,64]{3,2,1,0:T(8,128)(2,1)}, bf16[48,1,64,64]{3,2,1,0:T(8,128)(2,1)S(1)}, bf16[...) fusion(f32[64]{0:T(128)S(1)} %copy-done.10, f32[64]{0:T(128)S(1)} %copy-done.11, ...), kind=kLoop, calls=%fused_computation.10 | loop fusion | flops 4718592 | bytes 3933696 | tf_op jit(solution)/shard_map/convert.2
  157.9 2.1 convert_element_type.175
  160.0 1.7 pad_maximum_fusion.2
  161.7 2.1 convert_element_type.177
  163.8 4.8 %subtract_convert_fusion.1 = (bf16[48,1,64,64]{3,2,1,0:T(8,128)(2,1)}, bf16[48,1,64,64]{3,2,1,0:T(8,128)(2,1)}, bf16[48,1,64,64]{3,2,1,0:T(8,128)(2,1)S(1)}, bf1...) fusion(f32[64]{0:T(128)S(1)} %copy-done.14, ...), kind=kLoop, calls=%fused_computation.12 | loop fusion | flops 4718592 | bytes 3933696 | tf_op jit(solution)/shard_map/convert.4
  168.9 2.0 convert_element_type.179
  171.0 1.7 pad_maximum_fusion.4
  172.6 2.1 convert_element_type.181
  174.7 1.7 pad_maximum_fusion.5
  176.4 2.1 convert_element_type.183
  178.4 1.7 pad_maximum_fusion.6
  180.1 2.0 convert_element_type.185
  182.2 1.7 pad_maximum_fusion.7
  183.8 2.3 %convert_element_type.187 = bf16[48,8192]{1,0:T(8,128)(2,1)} reshape(bf16[48,2,64,64]{3,2,1,0:T(8,128)(2,1)S(1)} %pad_maximum_fusion.7) | data formatting | bytes 1572864 | tf_op jit(solution)/shard_map/convert_element_type | solution.py:46
  186.5 0.7 copy-done.1
  187.2 0.4 fusion.7
  187.7 0.4 fusion.6
  188.9 0.4 fusion.4
  190.1 0.4 fusion.2
  191.2 17.8 %pmax.7 = f32[64,48]{1,0:T(8,128)S(1)} all-reduce(f32[64,48]{1,0:T(8,128)S(1)} %fusion.1), channel_id=1, replica_groups=mesh['dom'=8,'rot'=4] {'rot'}, use_global_device_ids=true, to_apply=%region_5.6 | all-reduce | flops 3072 | bytes 24576 | tf_op jit(solution)/shard_map/pmax | solution.py:119
  209.0 0.6 constant_dynamic-slice_fusion.2
  (78 shorter events, 6.2 us)
Async XLA Ops:
  7.2 1.8 copy-start
  7.2 1.5 copy-start.22
  7.2 1.7 copy-start.24
  7.2 124.4 %all-reduce.5.cloned.1.call-start = ((), (), s32[]{:S(2)}) async-start(), calls=%async_computation | async-start | bytes 524288 | tf_op jit(solution)/shard_map/psum | solution.py:92
  9.4 0.7 copy-start.23
  10.9 59.0 %copy-start.9 = (u32[32]{0:T(128)S(1)}, u32[32]{0:T(128)}, u32[]{:S(2)}) copy-start(u32[32]{0:T(128)} %constant.99) | copy-start | bytes 388
  39.4 54.7 %collective-permute-start = (f32[8,8192]{1,0:T(8,128)S(1)}, f32[8,8192]{1,0:T(8,128)}, u32[]{:S(2)}, u32[]{:S(2)}) collective-permute-start(f32[8,8192]{1,0:T(8,128)S(1)} %fusion), channel_id=1, source_target_pairs={{0,4},{4,8},{8,12},{12,16},{16,20},{20,24},{24,28},{1,5},{5,9},{9,... | collective-permute-start | bytes 786440
  42.2 52.0 %collective-permute-start.1 = (f32[6,8192]{1,0:T(8,128)}, f32[6,8192]{1,0:T(8,128)}, u32[]{:S(2)}, u32[]{:S(2)}) collective-permute-start(f32[6,8192]{1,0:T(8,128)} %slice.16), channel_id=1, source_target_pairs={{0,8},{4,12},{8,16},{12,20},{16,24},{20,28},{1,9},{5,13},{9,17},{1... | collective-permute-start | bytes 589832
  133.8 13.4 %copy-start.8 = (bf16[6,8192]{1,0:T(8,128)(2,1)}, bf16[6,8192]{1,0:T(8,128)(2,1)S(1)}, u32[]{:S(2)}) copy-start(bf16[6,8192]{1,0:T(8,128)(2,1)S(1)} %divide_convert_fusion) | copy-start | bytes 294916
  151.3 1.4 copy-start.10
  151.4 1.4 copy-start.11
  151.4 1.4 copy-start.12
  151.4 1.4 copy-start.13
  151.4 1.4 copy-start.16
  151.4 1.4 copy-start.17
  161.7 2.1 copy-start.14
  161.7 2.1 copy-start.15
  161.7 2.1 copy-start.18
  161.7 2.1 copy-start.19
  161.7 2.1 copy-start.20
  161.7 2.1 copy-start.21
  186.1 1.1 copy-start.1
  186.1 1.6 copy-start.2
  187.2 1.2 copy-start.3
  187.7 1.2 copy-start.4
  188.4 1.2 copy-start.5
  188.9 1.2 copy-start.6
  189.6 1.2 copy-start.7
Sparse Core Ops, SparseCore 0:
  98.4 33.1 all-reduce.4
where the time goes:
time: 217 us; the launch traced here: 216 us
  blocking collectives  94.1 us (43%)
  local copies, waits for them, and re-layouts  33.6 us (15%)
  waiting for transfers between devices  32.1 us (15%)
  other arithmetic  31.7 us (15%)
  between operations  15.8 us (7%)
  matrix products  4.61 us (2%)
  starting transfers between devices  4.57 us (2%)
    unnamed x2, blocking collectives  53.4 us
    psum x1, waiting for transfers between devices, local(): numer, denom = lax.psum((numer, denom), 'rot')  32.1 us
    pmax x1, blocking collectives, local(): highest = lax.pmax(best, 'rot')  17.8 us
    convert_element_type x8, local copies, waits for them, and re-layouts, rotate_refs(): return turned.reshape(count, K).astype(jnp.bfloat16)  16 us
    another operation x3, other arithmetic  13.4 us
    psum x1, blocking collectives, local(): numer, denom = lax.psum((numer, denom), 'rot')  12 us
    all_gather x1, blocking collectives, local(): piece = lax.all_gather(refs, 'dom', axis=0, tiled=True)  10.9 us
    another operation x8, other arithmetic, rotate_refs(): jnp.stack([real_part * cosine - imag_part * sine, real_part * sine + imag...  9.3 us
  transfers between devices with their start and end apart: 3, of which 1 were waited for; matrix products, arithmetic and copies ran while one was open for 6% of the time, Pallas kernels for 0%

commit v1 on v0

v1 whole, which is shorter than its diff:
```python
import functools
import math

import jax
import jax.numpy as jnp
import numpy as np
from jax import lax
from jax.experimental import pallas as pl
from jax.experimental.pallas import tpu as pltpu
from jax.sharding import PartitionSpec as P

CYCLES = 64
MFREQ = 64
CLS = 6
BLOCKS = 8
ROWS = BLOCKS * CLS
FINE = 4
K = 2 * CYCLES * MFREQ
MESH = pl.DeviceIdType.MESH
F32 = jnp.float32
BF16 = jnp.bfloat16


def pieces(x):
    high = x.astype(BF16)
    rest = x - high.astype(F32)
    mid = rest.astype(BF16)
    low = (rest - mid.astype(F32)).astype(BF16)
    return high, mid, low


def exact_right(select, x):
    return sum(jnp.dot(select, part, preferred_element_type=F32) for part in pieces(x))


def exact_left(x, select):
    return sum(jnp.dot(part, select, preferred_element_type=F32) for part in pieces(x))


def iota(shape, dim):
    return lax.broadcasted_iota(jnp.int32, shape, dim)


def sixth(x):
    return lax.shift_right_logical(x * 10923, 16)


def ones_where(cond):
    return jnp.where(cond, 1.0, 0.0).astype(BF16)


def column_onehot(row, count):
    size = row.shape[1]
    wide = jnp.where(iota((count, size), 0) == row, 1.0, 0.0)
    return wide.T.astype(BF16)


def kernel(
    n_dom, n_rot,
    particles_ref, assign_ref, rot_ref, group_ref, table_ref, trig_ref,
    refs_ref, scores_ref,
    spec, sums, sums_in, plain_all, spread_mine, spread_in, normed, left, right,
    outgoing, incoming, norm_mine, norm_in,
    load_sem, a_send, a_recv, c_send, c_recv, s_send, s_recv, r_send, r_recv,
    e_send, e_recv, n_send, n_recv,
):
    me = lax.axis_index("dom")
    zed = lax.axis_index("rot")
    count = particles_ref.shape[0]
    total = trig_ref.shape[0] // 2
    share = count // n_rot
    coarse = total // FINE
    cyc = CYCLES // n_rot
    half = cyc * MFREQ
    lanes = half // 4
    tiles = ROWS // 8 * (lanes // 128)
    classes = CLS * n_dom
    groups = table_ref.shape[0]

    barrier = pltpu.get_barrier_semaphore()

    def dom_peer(step):
        return (lax.rem(me + step, n_dom), zed)

    def rot_peer(step):
        return (me, lax.rem(zed + step, n_rot))

    for step in range(1, n_dom):
        pl.semaphore_signal(barrier, inc=1, device_id=dom_peer(step), device_id_type=MESH)
    for step in range(1, n_rot):
        pl.semaphore_signal(barrier, inc=1, device_id=rot_peer(step), device_id_type=MESH)

    loads = []
    for part in range(2):
        start = pl.multiple_of(part * CYCLES * MFREQ + zed * half, 128)
        loads.append(
            pltpu.make_async_copy(
                particles_ref.at[:, pl.ds(start, half)], spec.at[part], load_sem.at[part]
            )
        )
        loads[-1].start()

    def widen(x):
        return x if lanes == 128 else jnp.concatenate([x] * (lanes // 128), axis=1)

    group_hot = column_onehot(group_ref[...], groups)
    rows = exact_right(group_hot, table_ref[...])
    spreader = ones_where(iota((CYCLES, half), 0) == zed * cyc + iota((CYCLES, half), 1) // MFREQ)
    factors = exact_left(rows, spreader)
    turn_hot = column_onehot(rot_ref[...], total)
    cosine = widen(exact_right(turn_hot, trig_ref[:total]))
    sine = widen(exact_right(turn_hot, trig_ref[total:]))

    labels = assign_ref[...]
    place = iota((n_dom * 8, count), 0)
    wanted = jnp.where((place & 7) < CLS, lax.shift_right_logical(place, 3) * CLS + (place & 7), -1)
    denom = exact_right(ones_where(wanted == labels), rows * rows)
    for owner in range(n_dom):
        sums[owner, tiles] = jnp.concatenate(
            [denom[owner * 8 : owner * 8 + 8], jnp.zeros((8, 128 - CYCLES), F32)], axis=1
        )

    place = iota((n_dom * ROWS, count), 0)
    six = sixth(place)
    block_of = six & (BLOCKS - 1)
    member = (lax.shift_right_logical(six, 3) * CLS + place - six * CLS) == labels

    for load in loads:
        load.wait()

    numer = jnp.zeros((n_dom * ROWS, lanes), F32)
    for block in range(BLOCKS):
        if block < 4:
            lane = slice(block * lanes, block * lanes + lanes)
            re = spec[0, :, lane].astype(F32)
            im = spec[1, :, lane].astype(F32)
            value = (re * cosine + im * sine) * factors[:, lane]
        else:
            lane = slice((block - 4) * lanes, (block - 4) * lanes + lanes)
            re = spec[0, :, lane].astype(F32)
            im = spec[1, :, lane].astype(F32)
            value = (im * cosine - re * sine) * factors[:, lane]
        chosen = ones_where(member & (block_of == block))
        stacked = jnp.concatenate([chosen] * 3, axis=1)
        numer += jnp.dot(
            stacked, jnp.concatenate(pieces(value), axis=0), preferred_element_type=F32
        )
    per_row = lanes // 128
    for owner in range(n_dom):
        for i in range(ROWS // 8):
            for j in range(per_row):
                first = owner * ROWS + i * 8
                sums[owner, i * per_row + j] = numer[first : first + 8, j * 128 : j * 128 + 128]

    pl.semaphore_wait(barrier, n_dom + n_rot - 2)

    a_copies = []
    for step in range(1, n_dom):
        a_copies.append(
            pltpu.make_async_remote_copy(
                src_ref=sums.at[lax.rem(me + step, n_dom)],
                dst_ref=sums_in.at[step - 1],
                send_sem=a_send.at[step - 1],
                recv_sem=a_recv.at[step - 1],
                device_id=dom_peer(step),
                device_id_type=MESH,
            )
        )
        a_copies[-1].start()

    for block in range(4):
        lane = slice(block * lanes, block * lanes + lanes)
        re = (spec[0, :, lane].astype(F32) * factors[:, lane]).astype(BF16).astype(F32)
        im = (spec[1, :, lane].astype(F32) * factors[:, lane]).astype(BF16).astype(F32)
        turned_re, turned_im = [], []
        for a in range(coarse):
            cos = widen(trig_ref[a * FINE : a * FINE + 1])
            sin = widen(trig_ref[total + a * FINE : total + a * FINE + 1])
            turned_re.append(re * cos + im * sin)
            turned_im.append(im * cos - re * sin)
        for part, turned in enumerate((turned_re, turned_im)):
            first = (part * 4 + block) * lanes
            for z in range(n_rot):
                left[z * 128 : z * 128 + 128, first : first + lanes] = jnp.concatenate(
                    [x[z * share : z * share + share] for x in turned], axis=0
                ).astype(BF16)

    for copy in a_copies:
        copy.wait_recv()

    whole = sums[me]
    for step in range(n_dom - 1):
        whole = whole + sums_in[step]
    numer = jnp.concatenate(
        [
            jnp.concatenate([whole[i * per_row + j] for j in range(per_row)], axis=1)
            for i in range(ROWS // 8)
        ],
        axis=0,
    )
    place = iota((ROWS, 8), 0)
    pick = ones_where(place - sixth(place) * CLS == iota((ROWS, 8), 1))
    denom = exact_right(pick, whole[tiles])
    cb = cyc // 4
    offset = iota((ROWS, 128), 1) - zed * cyc
    low = (sixth(iota((ROWS, 128), 0)) & 3) * cb
    denom = jnp.where((offset >= low) & (offset < low + cb), denom, 0.0)
    where_to = (iota((128, lanes), 0) & (cb - 1)) == iota((128, lanes), 1) // MFREQ
    denom = exact_left(denom, ones_where(where_to))
    plain = numer / (denom + 1.0)
    plain_all[me] = plain.astype(BF16)

    c_copies = []
    for step in range(1, n_dom):
        c_copies.append(
            pltpu.make_async_remote_copy(
                src_ref=plain_all.at[me],
                dst_ref=plain_all.at[me],
                send_sem=c_send.at[step - 1],
                recv_sem=c_recv.at[step - 1],
                device_id=dom_peer(step),
                device_id_type=MESH,
            )
        )
        c_copies[-1].start()

    squares = jnp.sum(plain * plain, axis=1, keepdims=True)
    place = iota((ROWS, ROWS), 0)
    other = iota((ROWS, ROWS), 1)
    same = ones_where(place - sixth(place) * CLS == other - sixth(other) * CLS)
    spread_mine[...] = exact_right(same, jnp.broadcast_to(squares, (ROWS, 128)))
    s_copies = []
    for step in range(1, n_rot):
        s_copies.append(
            pltpu.make_async_remote_copy(
                src_ref=spread_mine,
                dst_ref=spread_in.at[step - 1],
                send_sem=s_send.at[step - 1],
                recv_sem=s_recv.at[step - 1],
                device_id=rot_peer(step),
                device_id_type=MESH,
            )
        )
        s_copies[-1].start()
    for copy in s_copies:
        copy.wait_recv()
    spread = spread_mine[...]
    for step in range(n_rot - 1):
        spread = spread + spread_in[step]
    root = jnp.sqrt(spread / K + 1e-6)
    normed[zed] = (plain / widen(root)).astype(BF16)
    r_copies = []
    for step in range(1, n_rot):
        r_copies.append(
            pltpu.make_async_remote_copy(
                src_ref=normed.at[zed],
                dst_ref=normed.at[zed],
                send_sem=r_send.at[step - 1],
                recv_sem=r_recv.at[step - 1],
                device_id=rot_peer(step),
                device_id_type=MESH,
            )
        )
        r_copies[-1].start()

    for copy in c_copies:
        copy.wait_recv()

    gathered = plain_all[...].reshape(n_dom * ROWS, lanes)
    place = iota((classes, n_dom * ROWS), 0)
    owner = sixth(place)
    source = owner * ROWS + place - owner * CLS
    other = iota((classes, n_dom * ROWS), 1)
    blocks = [
        jnp.dot(
            ones_where(source + block * CLS == other), gathered, preferred_element_type=F32
        )
        for block in range(BLOCKS)
    ]
    for fine in range(FINE):
        cos = widen(trig_ref[fine : fine + 1])
        sin = widen(trig_ref[total + fine : total + fine + 1])
        for block in range(4):
            re, im = blocks[block], blocks[block + 4]
            at = slice(fine * classes, fine * classes + classes)
            right[at, block * lanes : block * lanes + lanes] = (re * cos - im * sin).astype(BF16)
            right[at, (block + 4) * lanes : (block + 4) * lanes + lanes] = (
                re * sin + im * cos
            ).astype(BF16)

    def partial(z):
        return lax.dot_general(
            right[...],
            left[pl.ds(pl.multiple_of(z * 128, 128), 128), :],
            (((1,), (1,)), ((), ())),
            preferred_element_type=F32,
        )

    e_copies = []
    for step in range(1, n_rot):
        outgoing[step - 1] = partial(lax.rem(zed + step, n_rot)).astype(BF16)
        e_copies.append(
            pltpu.make_async_remote_copy(
                src_ref=outgoing.at[step - 1],
                dst_ref=incoming.at[step - 1],
                send_sem=e_send.at[step - 1],
                recv_sem=e_recv.at[step - 1],
                device_id=rot_peer(step),
                device_id_type=MESH,
            )
        )
        e_copies[-1].start()
    found = partial(zed)

    squares = jnp.zeros((classes, lanes), F32)
    for block in blocks:
        squares = squares + block * block
    squares = jnp.broadcast_to(jnp.sum(squares, axis=1, keepdims=True), (classes, 128))
    norm_mine[...] = squares.T[:8]
    n_copies = []
    for step in range(1, n_rot):
        n_copies.append(
            pltpu.make_async_remote_copy(
                src_ref=norm_mine,
                dst_ref=norm_in.at[step - 1],
                send_sem=n_send.at[step - 1],
                recv_sem=n_recv.at[step - 1],
                device_id=rot_peer(step),
                device_id_type=MESH,
            )
        )
        n_copies[-1].start()

    for copy in r_copies:
        copy.wait_recv()
    for z in range(n_rot):
        mine = normed[z].astype(F32)
        for block in range(BLOCKS):
            first = (block // 4) * CYCLES * MFREQ + z * half + (block % 4) * lanes
            refs_ref[:, first : first + lanes] = mine[block * CLS : block * CLS + CLS].astype(BF16)

    for copy in n_copies:
        copy.wait_recv()
    spread = norm_mine[...]
    for step in range(n_rot - 1):
        spread = spread + norm_in[step]
    scale = (1.0 / math.sqrt(K)) / jnp.sqrt(spread / K + 1e-6)

    for step, copy in enumerate(e_copies):
        copy.wait_recv()
        found = found + incoming[step].astype(F32)
    best = found[:classes]
    for fine in range(1, FINE):
        best = jnp.maximum(best, found[fine * classes : fine * classes + classes])
    best = best.T
    top = best[:share]
    for a in range(1, coarse):
        top = jnp.maximum(top, best[a * share : a * share + share])
    scores_ref[...] = top * scale[:1]

    for copy in a_copies + c_copies + s_copies + r_copies + e_copies + n_copies:
        copy.wait_send()


def trig_table(total):
    freqs = np.arange(128) % MFREQ
    phase = (np.arange(total)[:, None] * freqs[None, :]) % total * (2.0 * math.pi / total)
    return np.concatenate([np.cos(phase), np.sin(phase)]).astype(np.float32)


def local(n_dom, n_rot, particles, assign, rot_index, group, ctf_table):
    count = particles.shape[0]
    total = 8 * n_rot
    share = count // n_rot
    lanes = CYCLES // n_rot * MFREQ // 4
    half = 4 * lanes
    tiles = ROWS // 8 * (lanes // 128)
    classes = CLS * n_dom
    vmem = pl.BlockSpec(memory_space=pltpu.VMEM)
    dma = pltpu.SemaphoreType.DMA
    dom, rot = dma((n_dom - 1,)), dma((n_rot - 1,))
    return pl.pallas_call(
        functools.partial(kernel, n_dom, n_rot),
        out_shape=(
            jax.ShapeDtypeStruct((CLS, K), BF16),
            jax.ShapeDtypeStruct((share, classes), F32),
        ),
        in_specs=[pl.BlockSpec(memory_space=pl.ANY)] + [vmem] * 5,
        out_specs=(vmem, vmem),
        scratch_shapes=[
            pltpu.VMEM((2, count, half), BF16),
            pltpu.VMEM((n_dom, tiles + 1, 8, 128), F32),
            pltpu.VMEM((n_dom - 1, tiles + 1, 8, 128), F32),
            pltpu.VMEM((n_dom, ROWS, lanes), BF16),
            pltpu.VMEM((ROWS, 128), F32),
            pltpu.VMEM((n_rot - 1, ROWS, 128), F32),
            pltpu.VMEM((n_rot, ROWS, lanes), BF16),
            pltpu.VMEM((n_rot * 128, 8 * lanes), BF16),
            pltpu.VMEM((FINE * classes, 8 * lanes), BF16),
            pltpu.VMEM((n_rot - 1, FINE * classes, 128), BF16),
            pltpu.VMEM((n_rot - 1, FINE * classes, 128), BF16),
            pltpu.VMEM((8, classes), F32),
            pltpu.VMEM((n_rot - 1, 8, classes), F32),
            dma((2,)),
            dom, dom, dom, dom, rot, rot, rot, rot, rot, rot, rot, rot,
        ],
        compiler_params=pltpu.CompilerParams(
            collective_id=0, has_side_effects=True, vmem_limit_bytes=48 * 1024 * 1024
        ),
    )(
        particles,
        assign.reshape(1, count),
        rot_index.reshape(1, count),
        group.reshape(1, count),
        ctf_table,
        jnp.asarray(trig_table(total)),
    )


def solution(mesh):
    sizes = dict(mesh.shape)
    in_specs = (P("dom", None), P("dom"), P("dom"), P("dom"), P())
    out_specs = (P("dom", None), P(("dom", "rot"), None))
    return jax.shard_map(
        functools.partial(local, sizes["dom"], sizes["rot"]),
        mesh=mesh, in_specs=in_specs, out_specs=out_specs, check_vma=False,
    )
```

time: 217 us -> 31.3 us (0.14)
  blocking collectives: 94.1 us -> 0 us
  waiting for transfers between devices: 32.1 us -> 0 us
  other arithmetic: 31.7 us -> 0 us
  local copies, waits for them, and re-layouts: 33.6 us -> 4.62 us
  Pallas kernels: 0 us -> 25.8 us
  between operations: 15.8 us -> 0.67 us
  matrix products: 4.61 us -> 0 us
  starting transfers between devices: 4.57 us -> 0 us
    unnamed x2 -> x0, blocking collectives: 53.4 us -> none
    psum x1 -> x0, waiting for transfers between devices: 32.1 us -> none  [local(): numer, denom = lax.psum((numer, denom), 'rot')]
    pallas_call x0 -> x1, Pallas kernels: none -> 25.8 us  [local(): pl.pallas_call(functools.partial(kernel, n_dom, n_rot), out_shape=(jax.Sh...]
    another operation x11 -> x0, other arithmetic: 22.7 us -> none
    pmax x1 -> x0, blocking collectives: 17.8 us -> none  [local(): highest = lax.pmax(best, 'rot')]
    convert_element_type x8 -> x0, local copies, waits for them, and re-layouts: 16 us -> none  [rotate_refs(): return turned.reshape(count, K).astype(jnp.bfloat16)]
    psum x1 -> x0, blocking collectives: 12 us -> none  [local(): numer, denom = lax.psum((numer, denom), 'rot')]
    all_gather x1 -> x0, blocking collectives: 10.9 us -> none  [local(): piece = lax.all_gather(refs, 'dom', axis=0, tiled=True)]
  transfers between devices with their start and end apart: 3 -> 0, of which waited for: 1 -> 0; matrix products, arithmetic and copies ran while one was open for 6% -> 0% of each run, Pallas kernels for 0% -> 0%
where the time goes in v1:
time: 31.3 us; the launch traced here: 31 us
  Pallas kernels  25.8 us (82%)
  local copies, waits for them, and re-layouts  4.62 us (15%)
  between operations  0.67 us (2%)
    pallas_call x1, Pallas kernels, local(): pl.pallas_call(functools.partial(kernel, n_dom, n_rot), out_shape=(jax.Sh...  25.8 us
    unnamed x14, local copies, waits for them, and re-layouts  4.62 us

profile of v1, /device:TPU:0, one launch (start us, length us, event | category | flops | bytes accessed | tf_op | source)
XLA Modules:
  0.0 31.0 jit_solution(10202623274842768739)
XLA Ops:
  0.6 0.0 copy-start.3
  0.6 0.0 copy-start.4
  0.7 0.0 copy-start.5
  0.7 0.6 %copy-done.3 = s32[64]{0:T(128)S(1)} copy-done((s32[64]{0:T(128)S(1)}, s32[64]{0:T(128)}, u32[]{:S(2)}) %copy-start.3) | copy-done | bytes 280
  1.3 0.0 copy-done.4
  1.3 0.0 copy-done.5
  1.3 0.0 copy-start
  1.3 1.2 %copy-done = bf16[64,8192]{1,0:T(8,128)(2,1)S(1)} copy-done((bf16[64,8192]{1,0:T(8,128)(2,1)S(1)}, bf16[64,8192]{1,0:T(8,128)(2,1)}, u32[]{:S(2)}) %copy-start) | copy-done | bytes 1048600
  2.5 0.0 copy-start.1
  2.5 0.8 %copy-done.1 = f32[64,128]{1,0:T(8,128)S(1)} copy-done((f32[64,128]{1,0:T(8,128)S(1)}, f32[64,128]{1,0:T(8,128)}, u32[]{:S(2)}) %copy-start.1) | copy-done | bytes 32792
  3.3 0.0 copy-start.2
  3.3 0.7 %copy-done.2 = f32[32,64]{1,0:T(8,128)S(1)} copy-done((f32[32,64]{1,0:T(8,128)S(1)}, f32[32,64]{1,0:T(8,128)}, u32[]{:S(2)}) %copy-start.2) | copy-done | bytes 8216
  4.0 25.8 %shard_map.77 = (bf16[6,8192]{1,0:T(8,128)(2,1)S(1)}, f32[16,48]{1,0:T(8,128)S(1)}) custom-call(bf16[64,8192]{1,0:T(8,128)(2,1)S(1)} %copy-done, s32[1,64]{1,0:T(1,128)S(1)} %bitcast.3, s32[1,64]{1,0:T(1,128)S(1)} %bitcast.4, s32[1,64]{1,0:T(1,128)S(1)} %bitcast.5, f32[32,64]{1,0:T(8,128)S(1)} %copy-done.2, f32[64,128]{1,0:T(8,128)S(1)} %copy-done.1), custom_call_target="tpu_custom_call" | custom-call | tf_op jit(solution)/shard_map/pallas_call | solution.py:382
  29.8 0.7 %copy.10 = bf16[6,8192]{1,0:T(8,128)(2,1)} copy(bf16[6,8192]{1,0:T(8,128)(2,1)S(1)} %get-tuple-element.4) | data formatting | bytes 196608
  30.4 0.6 %copy.11 = f32[16,48]{1,0:T(8,128)} copy(f32[16,48]{1,0:T(8,128)S(1)} %get-tuple-element.5) | data formatting | bytes 6144
Async XLA Ops:
  0.6 0.7 %copy-start.3 = (s32[64]{0:T(128)S(1)}, s32[64]{0:T(128)}, u32[]{:S(2)}) copy-start(s32[64]{0:T(128)} %param.7) | copy-start | bytes 772
  0.6 0.7 %copy-start.4 = (s32[64]{0:T(128)S(1)}, s32[64]{0:T(128)}, u32[]{:S(2)}) copy-start(s32[64]{0:T(128)} %param.8) | copy-start | bytes 772
  0.7 0.7 %copy-start.5 = (s32[64]{0:T(128)S(1)}, s32[64]{0:T(128)}, u32[]{:S(2)}) copy-start(s32[64]{0:T(128)} %param.9) | copy-start | bytes 772
  1.3 1.2 %copy-start = (bf16[64,8192]{1,0:T(8,128)(2,1)S(1)}, bf16[64,8192]{1,0:T(8,128)(2,1)}, u32[]{:S(2)}) copy-start(bf16[64,8192]{1,0:T(8,128)(2,1)} %particles_ref.1) | copy-start | bytes 3145732
  2.5 0.8 %copy-start.1 = (f32[64,128]{1,0:T(8,128)S(1)}, f32[64,128]{1,0:T(8,128)}, u32[]{:S(2)}) copy-start(f32[64,128]{1,0:T(8,128)} %constant.2.clone.trig_ref) | copy-start | bytes 98308
  3.3 0.7 %copy-start.2 = (f32[32,64]{1,0:T(8,128)S(1)}, f32[32,64]{1,0:T(8,128)}, u32[]{:S(2)}) copy-start(f32[32,64]{1,0:T(8,128)} %table_ref.1) | copy-start | bytes 24580

commit v2 on v1

v2 whole, which is shorter than its diff:
```python
import functools
import math

import jax
import jax.numpy as jnp
import numpy as np
from jax import lax
from jax.experimental import pallas as pl
from jax.experimental.pallas import tpu as pltpu
from jax.sharding import PartitionSpec as P

CYCLES = 64
MFREQ = 64
CLS = 6
BLOCKS = 8
ROWS = BLOCKS * CLS
FINE = 4
K = 2 * CYCLES * MFREQ
MESH = pl.DeviceIdType.MESH
F32 = jnp.float32
BF16 = jnp.bfloat16


def pieces(x):
    high = x.astype(BF16)
    rest = x - high.astype(F32)
    mid = rest.astype(BF16)
    low = (rest - mid.astype(F32)).astype(BF16)
    return high, mid, low


def stacked(x):
    return jnp.concatenate(pieces(x), axis=0)


def iota(shape, dim):
    return lax.broadcasted_iota(jnp.int32, shape, dim)


def ones_where(cond):
    return jnp.where(cond, 1.0, 0.0).astype(BF16)


def dot(x, y):
    return jnp.dot(x, y, preferred_element_type=F32)


def column_onehot(row, count):
    shape = (3 * count, row.shape[1])
    return jnp.where((iota(shape, 0) & (count - 1)) == row, 1.0, 0.0).T.astype(BF16)


def each_row(tile):
    return jnp.concatenate([jnp.broadcast_to(tile[c : c + 1], (8, 128)) for c in range(CLS)], axis=0)


def kernel(
    n_dom, n_rot,
    particles_hbm, assign_hbm, rot_hbm, group_hbm, table_hbm, trig_hbm,
    refs_ref, scores_ref,
    spec, assign_ref, rot_ref, group_ref, table_ref, trig_ref,
    sums, sums_in, plain_all, wide, spread_mine, spread_in, normed, left, right,
    outgoing, incoming, norm_mine, norm_in,
    load_sem, a_send, a_recv, c_send, c_recv, s_send, s_recv, r_send, r_recv,
    e_send, e_recv, n_send, n_recv,
):
    me = lax.axis_index("dom")
    zed = lax.axis_index("rot")
    count = spec.shape[1]
    total = trig_ref.shape[0]
    share = count // n_rot
    coarse = total // FINE
    cyc = CYCLES // n_rot
    half = cyc * MFREQ
    lanes = half // 4
    per_row = lanes // 128
    classes = CLS * n_dom
    groups = table_ref.shape[0]

    barrier = pltpu.get_barrier_semaphore()

    def dom_peer(step):
        return (lax.rem(me + step, n_dom), zed)

    def rot_peer(step):
        return (me, lax.rem(zed + step, n_rot))

    for step in range(1, n_dom):
        pl.semaphore_signal(barrier, inc=1, device_id=dom_peer(step), device_id_type=MESH)
    for step in range(1, n_rot):
        pl.semaphore_signal(barrier, inc=1, device_id=rot_peer(step), device_id_type=MESH)

    pairs = [(group_hbm, group_ref), (table_hbm, table_ref), (rot_hbm, rot_ref)]
    pairs += [(trig_hbm, trig_ref), (assign_hbm, assign_ref)]
    for part in range(2):
        start = pl.multiple_of(part * CYCLES * MFREQ + zed * half, 128)
        pairs.append((particles_hbm.at[:, pl.ds(start, half)], spec.at[part]))
    loads = [pltpu.make_async_copy(x, y, load_sem.at[i]) for i, (x, y) in enumerate(pairs)]
    for load in loads:
        load.start()

    def widen(x):
        return x if per_row == 1 else jnp.concatenate([x] * per_row, axis=1)

    def side_by_side(take):
        tiles = [take(i) for i in range(per_row)]
        return tiles[0] if per_row == 1 else jnp.concatenate(tiles, axis=1)

    shape = (3 * CYCLES, half)
    spreader = ones_where((iota(shape, 0) & (CYCLES - 1)) == zed * cyc + iota(shape, 1) // MFREQ)
    loads[0].wait()
    loads[1].wait()
    rows = dot(column_onehot(group_ref[...], groups), stacked(table_ref[...]))
    factors = dot(jnp.concatenate(pieces(rows), axis=1), spreader)
    loads[2].wait()
    loads[3].wait()
    turns = dot(column_onehot(rot_ref[...], total), stacked(trig_ref[...]))
    cosine, sine = widen(turns[:, :128]), widen(turns[:, 128:])

    loads[4].wait()
    labels = jnp.concatenate([assign_ref[...]] * 3, axis=1)
    place = iota((classes, 3 * count), 0)
    member = ones_where((place & (n_dom - 1)) * CLS + place // n_dom == labels)
    denom = dot(member, stacked(rows * rows))
    denom = jnp.concatenate([denom, jnp.zeros((classes, 128 - CYCLES), F32)], axis=1)
    for c in range(CLS):
        at = pl.ds(ROWS + c, n_dom, stride=ROWS + 8)
        sums[0, at, :] = denom[c * n_dom : c * n_dom + n_dom]

    loads[5].wait()
    loads[6].wait()
    for block in range(4):
        lane = slice(block * lanes, block * lanes + lanes)
        re = spec[0, :, lane].astype(F32)
        im = spec[1, :, lane].astype(F32)
        both = (re * cosine + im * sine, im * cosine - re * sine)
        for part, value in enumerate(both):
            numer = dot(member, stacked(value * factors[:, lane]))
            for c in range(CLS):
                at = pl.ds(c * 8 + part * 4 + block, n_dom, stride=ROWS + 8)
                for i in range(per_row):
                    sums[i, at, :] = numer[c * n_dom : c * n_dom + n_dom, i * 128 : i * 128 + 128]

    pl.semaphore_wait(barrier, n_dom + n_rot - 2)

    def owned(owner):
        return sums.at[:, pl.ds(pl.multiple_of(owner * (ROWS + 8), 8), ROWS + 8), :]

    a_copies = []
    for step in range(1, n_dom):
        a_copies.append(
            pltpu.make_async_remote_copy(
                src_ref=owned(lax.rem(me + step, n_dom)),
                dst_ref=sums_in.at[step - 1],
                send_sem=a_send.at[step - 1],
                recv_sem=a_recv.at[step - 1],
                device_id=dom_peer(step),
                device_id_type=MESH,
            )
        )
        a_copies[-1].start()

    for block in range(4):
        lane = slice(block * lanes, block * lanes + lanes)
        re = (spec[0, :, lane].astype(F32) * factors[:, lane]).astype(BF16).astype(F32)
        im = (spec[1, :, lane].astype(F32) * factors[:, lane]).astype(BF16).astype(F32)
        turned_re, turned_im = [], []
        for a in range(coarse):
            cos = widen(trig_ref[a * FINE : a * FINE + 1, :128])
            sin = widen(trig_ref[a * FINE : a * FINE + 1, 128:])
            turned_re.append(re * cos + im * sin)
            turned_im.append(im * cos - re * sin)
        for part, turned in enumerate((turned_re, turned_im)):
            first = (part * 4 + block) * lanes
            for z in range(n_rot):
                left[z * 128 : z * 128 + 128, first : first + lanes] = jnp.concatenate(
                    [x[z * share : z * share + share] for x in turned], axis=0
                ).astype(BF16)

    cb = cyc // 4
    offset = iota((ROWS, 128), 1) - zed * cyc
    low = (iota((ROWS, 128), 0) & 3) * cb
    shape = (3 * 128, lanes)
    spreader = ones_where((iota(shape, 0) & (cb - 1)) == iota(shape, 1) // MFREQ)

    for copy in a_copies:
        copy.wait_recv()

    whole = owned(me)[...]
    for step in range(n_dom - 1):
        whole = whole + sums_in[step]
    numer = side_by_side(lambda i: whole[i, :ROWS])
    denom = jnp.where((offset >= low) & (offset < low + cb), each_row(whole[0, ROWS:]), 0.0)
    denom = dot(jnp.concatenate(pieces(denom), axis=1), spreader)
    plain = numer / (denom + 1.0)
    plain_all[me] = plain.astype(BF16)

    c_copies = []
    for step in range(1, n_dom):
        c_copies.append(
            pltpu.make_async_remote_copy(
                src_ref=plain_all.at[me],
                dst_ref=plain_all.at[me],
                send_sem=c_send.at[step - 1],
                recv_sem=c_recv.at[step - 1],
                device_id=dom_peer(step),
                device_id_type=MESH,
            )
        )
        c_copies[-1].start()

    squares = jnp.sum((plain * plain).reshape(CLS, 8, lanes), axis=1)
    squares = jnp.broadcast_to(jnp.sum(squares, axis=1, keepdims=True), (CLS, 128))
    spread_mine[...] = jnp.concatenate([squares, jnp.zeros((8 - CLS, 128), F32)], axis=0)
    s_copies = []
    for step in range(1, n_rot):
        s_copies.append(
            pltpu.make_async_remote_copy(
                src_ref=spread_mine,
                dst_ref=spread_in.at[step - 1],
                send_sem=s_send.at[step - 1],
                recv_sem=s_recv.at[step - 1],
                device_id=rot_peer(step),
                device_id_type=MESH,
            )
        )
        s_copies[-1].start()
    for copy in s_copies:
        copy.wait_recv()
    spread = spread_mine[...]
    for step in range(n_rot - 1):
        spread = spread + spread_in[step]
    root = each_row(jnp.sqrt(spread / K + 1e-6))
    normed[zed] = (plain / widen(root)).astype(BF16)
    r_copies = []
    for step in range(1, n_rot):
        r_copies.append(
            pltpu.make_async_remote_copy(
                src_ref=normed.at[zed],
                dst_ref=normed.at[zed],
                send_sem=r_send.at[step - 1],
                recv_sem=r_recv.at[step - 1],
                device_id=rot_peer(step),
                device_id_type=MESH,
            )
        )
        r_copies[-1].start()

    for copy in c_copies:
        copy.wait_recv()

    for i in range(per_row):
        wide[i] = plain_all[:, :, i * 128 : i * 128 + 128].astype(F32).reshape(classes * 8, 128)
    blocks = [
        side_by_side(lambda i: wide[i, pl.ds(block, classes, stride=8), :])
        for block in range(BLOCKS)
    ]
    for fine in range(FINE):
        cos = widen(trig_ref[fine : fine + 1, :128])
        sin = widen(trig_ref[fine : fine + 1, 128:])
        for block in range(4):
            re, im = blocks[block], blocks[block + 4]
            at = slice(fine * classes, fine * classes + classes)
            right[at, block * lanes : block * lanes + lanes] = (re * cos - im * sin).astype(BF16)
            right[at, (block + 4) * lanes : (block + 4) * lanes + lanes] = (
                re * sin + im * cos
            ).astype(BF16)

    def partial(z):
        return lax.dot_general(
            right[...],
            left[pl.ds(pl.multiple_of(z * 128, 128), 128), :],
            (((1,), (1,)), ((), ())),
            preferred_element_type=F32,
        )

    e_copies = []
    for step in range(1, n_rot):
        outgoing[step - 1] = partial(lax.rem(zed + step, n_rot)).astype(BF16)
        e_copies.append(
            pltpu.make_async_remote_copy(
                src_ref=outgoing.at[step - 1],
                dst_ref=incoming.at[step - 1],
                send_sem=e_send.at[step - 1],
                recv_sem=e_recv.at[step - 1],
                device_id=rot_peer(step),
                device_id_type=MESH,
            )
        )
        e_copies[-1].start()

    squares = jnp.zeros((classes, lanes), F32)
    for block in range(BLOCKS):
        x = side_by_side(lambda i: wide[i, pl.ds(block, classes, stride=8), :])
        squares = squares + x * x
    squares = jnp.broadcast_to(jnp.sum(squares, axis=1, keepdims=True), (classes, 128))
    norm_mine[...] = squares.T[:8]
    n_copies = []
    for step in range(1, n_rot):
        n_copies.append(
            pltpu.make_async_remote_copy(
                src_ref=norm_mine,
                dst_ref=norm_in.at[step - 1],
                send_sem=n_send.at[step - 1],
                recv_sem=n_recv.at[step - 1],
                device_id=rot_peer(step),
                device_id_type=MESH,
            )
        )
        n_copies[-1].start()
    found = partial(zed)

    for copy in r_copies:
        copy.wait_recv()
    for z in range(n_rot):
        for i in range(per_row):
            wide[i, :ROWS] = normed[z, :, i * 128 : i * 128 + 128].astype(F32)
            for block in range(BLOCKS):
                first = (block // 4) * CYCLES * MFREQ + z * half + (block % 4) * lanes + i * 128
                refs_ref[:, first : first + 128] = wide[i, pl.ds(block, CLS, stride=8), :].astype(
                    BF16
                )

    for copy in n_copies:
        copy.wait_recv()
    spread = norm_mine[...]
    for step in range(n_rot - 1):
        spread = spread + norm_in[step]
    scale = (1.0 / math.sqrt(K)) / jnp.sqrt(spread / K + 1e-6)

    for step, copy in enumerate(e_copies):
        copy.wait_recv()
        found = found + incoming[step].astype(F32)
    best = found[:classes]
    for fine in range(1, FINE):
        best = jnp.maximum(best, found[fine * classes : fine * classes + classes])
    best = best.T
    top = best[:share]
    for a in range(1, coarse):
        top = jnp.maximum(top, best[a * share : a * share + share])
    scores_ref[...] = top * scale[:1]

    for copy in a_copies + c_copies + s_copies + r_copies + e_copies + n_copies:
        copy.wait_send()


def trig_table(total):
    freqs = np.arange(128) % MFREQ
    phase = (np.arange(total)[:, None] * freqs[None, :]) % total * (2.0 * math.pi / total)
    return np.concatenate([np.cos(phase), np.sin(phase)], axis=1).astype(np.float32)


def local(n_dom, n_rot, particles, assign, rot_index, group, ctf_table):
    count = particles.shape[0]
    total = 8 * n_rot
    share = count // n_rot
    lanes = CYCLES // n_rot * MFREQ // 4
    half = 4 * lanes
    per_row = lanes // 128
    classes = CLS * n_dom
    vmem = pl.BlockSpec(memory_space=pltpu.VMEM)
    dma = pltpu.SemaphoreType.DMA
    dom, rot = dma((n_dom - 1,)), dma((n_rot - 1,))
    return pl.pallas_call(
        functools.partial(kernel, n_dom, n_rot),
        out_shape=(
            jax.ShapeDtypeStruct((CLS, K), BF16),
            jax.ShapeDtypeStruct((share, classes), F32),
        ),
        in_specs=[pl.BlockSpec(memory_space=pltpu.HBM)] * 6,
        out_specs=(vmem, vmem),
        scratch_shapes=[
            pltpu.VMEM((2, count, half), BF16),
            pltpu.VMEM((1, count), jnp.int32),
            pltpu.VMEM((1, count), jnp.int32),
            pltpu.VMEM((1, count), jnp.int32),
            pltpu.VMEM(ctf_table.shape, F32),
            pltpu.VMEM((total, 256), F32),
            pltpu.VMEM((per_row, n_dom * (ROWS + 8), 128), F32),
            pltpu.VMEM((n_dom - 1, per_row, ROWS + 8, 128), F32),
            pltpu.VMEM((n_dom, ROWS, lanes), BF16),
            pltpu.VMEM((per_row, n_dom * ROWS, 128), F32),
            pltpu.VMEM((8, 128), F32),
            pltpu.VMEM((n_rot - 1, 8, 128), F32),
            pltpu.VMEM((n_rot, ROWS, lanes), BF16),
            pltpu.VMEM((n_rot * 128, 8 * lanes), BF16),
            pltpu.VMEM((FINE * classes, 8 * lanes), BF16),
            pltpu.VMEM((n_rot - 1, FINE * classes, 128), BF16),
            pltpu.VMEM((n_rot - 1, FINE * classes, 128), BF16),
            pltpu.VMEM((8, classes), F32),
            pltpu.VMEM((n_rot - 1, 8, classes), F32),
            dma((7,)),
            dom, dom, dom, dom, rot, rot, rot, rot, rot, rot, rot, rot,
        ],
        compiler_params=pltpu.CompilerParams(
            collective_id=0, has_side_effects=True, vmem_limit_bytes=48 * 1024 * 1024
        ),
    )(
        *(
            pltpu.with_memory_space_constraint(x, pltpu.HBM)
            for x in (
                particles,
                assign.reshape(1, count),
                rot_index.reshape(1, count),
                group.reshape(1, count),
                ctf_table,
                jnp.asarray(trig_table(total)),
            )
        )
    )


def solution(mesh):
    sizes = dict(mesh.shape)
    in_specs = (P("dom", None), P("dom"), P("dom"), P("dom"), P())
    out_specs = (P("dom", None), P(("dom", "rot"), None))
    return jax.shard_map(
        functools.partial(local, sizes["dom"], sizes["rot"]),
        mesh=mesh, in_specs=in_specs, out_specs=out_specs, check_vma=False,
    )
```

time: 31.3 us -> 27.4 us (0.88)
  local copies, waits for them, and re-layouts: 4.62 us -> 1.26 us
  Pallas kernels: 25.8 us -> 25.3 us
    unnamed x14 -> x2, local copies, waits for them, and re-layouts: 4.62 us -> 1.26 us
    pallas_call x1, Pallas kernels: 25.8 us -> 25.3 us  [local(): pl.pallas_call(functools.partial(kernel, n_dom, n_rot), out_shape=(jax.Sh...]
where the time goes in v2:
time: 27.4 us; the launch traced here: 27.2 us
  Pallas kernels  25.3 us (92%)
  local copies, waits for them, and re-layouts  1.26 us (5%)
  between operations  0.64 us (2%)
    pallas_call x1, Pallas kernels, local(): pl.pallas_call(functools.partial(kernel, n_dom, n_rot), out_shape=(jax.Sh...  25.3 us
    unnamed x2, local copies, waits for them, and re-layouts  1.26 us

profile of v2, /device:TPU:0, one launch (start us, length us, event | category | flops | bytes accessed | tf_op | source)
XLA Modules:
  0.0 27.2 jit_solution(4865879931330057034)
XLA Ops:
  0.6 25.3 %shard_map.77 = (bf16[6,8192]{1,0:T(8,128)(2,1)S(1)}, f32[16,48]{1,0:T(8,128)S(1)}) custom-call(bf16[64,8192]{1,0:T(8,128)(2,1)} %particles_hbm.1, s32[1,64]{1,0:T(1,128)} %bitcast.3, s32[1,64]{1,0:T(1,128)} %bitcast.4, s32[1,64]{1,0:T(1,128)} %bitcast.5, f32[32,64]{1,0:T(8,128)} %table_hbm.1, f32[32,256]{1,0:T(8,128)} %constant.2.clone.trig_hbm), custom_call_target="tpu_custom_call" | custom-call | tf_op jit(solution)/shard_map/pallas_call | solution.py:364
  26.0 0.7 %copy.10 = bf16[6,8192]{1,0:T(8,128)(2,1)} copy(bf16[6,8192]{1,0:T(8,128)(2,1)S(1)} %get-tuple-element.4) | data formatting | bytes 196608
  26.6 0.6 %copy.11 = f32[16,48]{1,0:T(8,128)} copy(f32[16,48]{1,0:T(8,128)S(1)} %get-tuple-element.5) | data formatting | bytes 6144

commit v3 on v2

v3 whole, which is shorter than its diff:
```python
import functools
import math

import jax
import jax.numpy as jnp
import numpy as np
from jax import lax
from jax.experimental import pallas as pl
from jax.experimental.pallas import tpu as pltpu
from jax.sharding import PartitionSpec as P

CYCLES = 64
MFREQ = 64
CLS = 6
BLOCKS = 8
ROWS = BLOCKS * CLS
FINE = 4
K = 2 * CYCLES * MFREQ
MESH = pl.DeviceIdType.MESH
F32 = jnp.float32
BF16 = jnp.bfloat16


def pieces(x):
    high = x.astype(BF16)
    rest = x - high.astype(F32)
    mid = rest.astype(BF16)
    low = (rest - mid.astype(F32)).astype(BF16)
    return high, mid, low


def stacked(x):
    return jnp.concatenate(pieces(x), axis=0)


def iota(shape, dim):
    return lax.broadcasted_iota(jnp.int32, shape, dim)


def ones_where(cond):
    return jnp.where(cond, 1.0, 0.0).astype(BF16)


def dot(x, y):
    return jnp.dot(x, y, preferred_element_type=F32)


def column_onehot(row, count):
    shape = (3 * count, row.shape[1])
    return jnp.where((iota(shape, 0) & (count - 1)) == row, 1.0, 0.0).T.astype(BF16)


def each_row(tile):
    return jnp.concatenate([jnp.broadcast_to(tile[c : c + 1], (8, 128)) for c in range(CLS)], axis=0)


def kernel(
    n_dom, n_rot,
    particles_hbm, assign_hbm, rot_hbm, group_hbm, table_hbm, trig_hbm,
    refs_ref, scores_ref,
    spec, assign_ref, rot_ref, group_ref, table_ref, trig_ref,
    sums, sums_in, plain_all, wide, spread_mine, spread_in, normed, left, right,
    earlier, outgoing, incoming, norm_mine, norm_in,
    load_sem, a_send, a_recv, c_send, c_recv, s_send, s_recv, r_send, r_recv,
    e_send, e_recv, n_send, n_recv,
):
    me = lax.axis_index("dom")
    zed = lax.axis_index("rot")
    count = spec.shape[1]
    total = trig_ref.shape[0]
    share = count // n_rot
    coarse = total // FINE
    cyc = CYCLES // n_rot
    half = cyc * MFREQ
    lanes = half // 4
    per_row = lanes // 128
    classes = CLS * n_dom
    groups = table_ref.shape[0]

    barrier = pltpu.get_barrier_semaphore()

    def dom_peer(step):
        return (lax.rem(me + step, n_dom), zed)

    def rot_peer(step):
        return (me, lax.rem(zed + step, n_rot))

    for step in range(1, n_dom):
        pl.semaphore_signal(barrier, inc=1, device_id=dom_peer(step), device_id_type=MESH)
    for step in range(1, n_rot):
        pl.semaphore_signal(barrier, inc=1, device_id=rot_peer(step), device_id_type=MESH)

    pairs = [(group_hbm, group_ref), (table_hbm, table_ref), (rot_hbm, rot_ref)]
    pairs += [(trig_hbm, trig_ref), (assign_hbm, assign_ref)]
    for part in range(2):
        start = pl.multiple_of(part * CYCLES * MFREQ + zed * half, 128)
        pairs.append((particles_hbm.at[:, pl.ds(start, half)], spec.at[part]))
    loads = [pltpu.make_async_copy(x, y, load_sem.at[i]) for i, (x, y) in enumerate(pairs)]
    for load in loads:
        load.start()

    shape = (3 * CYCLES, half)
    spreader = ones_where((iota(shape, 0) & (CYCLES - 1)) == zed * cyc + iota(shape, 1) // MFREQ)
    loads[0].wait()
    loads[1].wait()
    rows = dot(column_onehot(group_ref[...], groups), stacked(table_ref[...]))
    factors = dot(jnp.concatenate(pieces(rows), axis=1), spreader)
    loads[2].wait()
    loads[3].wait()
    turns = dot(column_onehot(rot_ref[...], total), stacked(trig_ref[...]))
    cosine, sine = turns[:, :128], turns[:, 128:]

    loads[4].wait()
    labels = jnp.concatenate([assign_ref[...]] * 3, axis=1)
    place = iota((classes, 3 * count), 0)
    member = ones_where((place & (n_dom - 1)) * CLS + place // n_dom == labels)
    denom = dot(member, stacked(rows * rows))
    denom = jnp.concatenate([denom, jnp.zeros((classes, 128 - CYCLES), F32)], axis=1)
    for c in range(CLS):
        at = pl.ds(ROWS + c, n_dom, stride=ROWS + 8)
        sums[0, at, :] = denom[c * n_dom : c * n_dom + n_dom]

    def message(part, owner):
        first = pl.multiple_of(owner * (ROWS + 8), 8)
        return sums.at[part, pl.ds(first, ROWS + 8 if part == 0 else ROWS), :]

    def landing(part, step):
        return sums_in.at[step - 1, part, pl.ds(0, ROWS + 8 if part == 0 else ROWS), :]

    def lane_tile(block, part):
        first = block * lanes + part * 128
        return slice(first, first + 128)

    loads[5].wait()
    loads[6].wait()
    a_copies = []
    for part in range(per_row):
        for block in range(4):
            lane = lane_tile(block, part)
            re = spec[0, :, lane].astype(F32)
            im = spec[1, :, lane].astype(F32)
            both = [re * cosine + im * sine, im * cosine - re * sine]
            value = jnp.concatenate([x * factors[:, lane] for x in both], axis=1)
            numer = dot(member, stacked(value))
            for c in range(CLS):
                for i in range(2):
                    at = pl.ds(c * 8 + i * 4 + block, n_dom, stride=ROWS + 8)
                    sums[part, at, :] = numer[
                        c * n_dom : c * n_dom + n_dom, i * 128 : i * 128 + 128
                    ]
        if part == 0:
            pl.semaphore_wait(barrier, n_dom + n_rot - 2)
        group_copies = []
        for step in range(1, n_dom):
            group_copies.append(
                pltpu.make_async_remote_copy(
                    src_ref=message(part, lax.rem(me + step, n_dom)),
                    dst_ref=landing(part, step),
                    send_sem=a_send.at[part, step - 1],
                    recv_sem=a_recv.at[part, step - 1],
                    device_id=dom_peer(step),
                    device_id_type=MESH,
                )
            )
            group_copies[-1].start()
        a_copies.append(group_copies)

    for part in range(per_row):
        for block in range(4):
            lane = lane_tile(block, part)
            re = (spec[0, :, lane].astype(F32) * factors[:, lane]).astype(BF16).astype(F32)
            im = (spec[1, :, lane].astype(F32) * factors[:, lane]).astype(BF16).astype(F32)
            turned_re, turned_im = [], []
            for a in range(coarse):
                cos = trig_ref[a * FINE : a * FINE + 1, :128]
                sin = trig_ref[a * FINE : a * FINE + 1, 128:]
                turned_re.append(re * cos + im * sin)
                turned_im.append(im * cos - re * sin)
            for i, turned in enumerate((turned_re, turned_im)):
                first = (i * 4 + block) * 128
                for z in range(n_rot):
                    left[part, z * 128 : z * 128 + 128, first : first + 128] = jnp.concatenate(
                        [x[z * share : z * share + share] for x in turned], axis=0
                    ).astype(BF16)

    cb = cyc // 4
    offset = iota((ROWS, 128), 1) - zed * cyc
    low = (iota((ROWS, 128), 0) & 3) * cb
    shape = (3 * 128, lanes)
    spreader = ones_where((iota(shape, 0) & (cb - 1)) == iota(shape, 1) // MFREQ)

    c_copies = []
    plain = []
    for part in range(per_row):
        for copy in a_copies[part]:
            copy.wait_recv()
        whole = message(part, me)[...]
        for step in range(1, n_dom):
            whole = whole + landing(part, step)[...]
        if part == 0:
            denom = jnp.where(
                (offset >= low) & (offset < low + cb), each_row(whole[ROWS:]), 0.0
            )
            denom = dot(jnp.concatenate(pieces(denom), axis=1), spreader) + 1.0
        plain.append(whole[:ROWS] / denom[:, part * 128 : part * 128 + 128])
        plain_all[part, me] = plain[-1].astype(BF16)
        group_copies = []
        for step in range(1, n_dom):
            group_copies.append(
                pltpu.make_async_remote_copy(
                    src_ref=plain_all.at[part, me],
                    dst_ref=plain_all.at[part, me],
                    send_sem=c_send.at[part, step - 1],
                    recv_sem=c_recv.at[part, step - 1],
                    device_id=dom_peer(step),
                    device_id_type=MESH,
                )
            )
            group_copies[-1].start()
        c_copies.append(group_copies)

    squares = sum(jnp.sum((x * x).reshape(CLS, 8, 128), axis=1) for x in plain)
    squares = jnp.broadcast_to(jnp.sum(squares, axis=1, keepdims=True), (CLS, 128))
    spread_mine[...] = jnp.concatenate([squares, jnp.zeros((8 - CLS, 128), F32)], axis=0)
    s_copies = []
    for step in range(1, n_rot):
        s_copies.append(
            pltpu.make_async_remote_copy(
                src_ref=spread_mine,
                dst_ref=spread_in.at[step - 1],
                send_sem=s_send.at[step - 1],
                recv_sem=s_recv.at[step - 1],
                device_id=rot_peer(step),
                device_id_type=MESH,
            )
        )
        s_copies[-1].start()

    def turn_references(part):
        for copy in c_copies[part]:
            copy.wait_recv()
        wide[part] = plain_all[part].astype(F32).reshape(classes * 8, 128)
        blocks = [wide[part, pl.ds(block, classes, stride=8), :] for block in range(BLOCKS)]
        for fine in range(FINE):
            cos = trig_ref[fine : fine + 1, :128]
            sin = trig_ref[fine : fine + 1, 128:]
            at = slice(fine * classes, fine * classes + classes)
            for block in range(4):
                re, im = blocks[block], blocks[block + 4]
                lane = slice(block * 128, block * 128 + 128)
                right[part, at, lane] = (re * cos - im * sin).astype(BF16)
                lane = slice(block * 128 + 512, block * 128 + 640)
                right[part, at, lane] = (re * sin + im * cos).astype(BF16)

    def product(part, rows):
        return lax.dot_general(
            right[part], rows, (((1,), (1,)), ((), ())), preferred_element_type=F32
        )

    for part in range(per_row - 1):
        turn_references(part)
        found = product(part, left[part])
        for z in range(n_rot):
            first = found[:, z * 128 : z * 128 + 128]
            earlier[z] = first if part == 0 else earlier[z] + first

    for copy in s_copies:
        copy.wait_recv()
    spread = spread_mine[...]
    for step in range(n_rot - 1):
        spread = spread + spread_in[step]
    root = each_row(jnp.sqrt(spread / K + 1e-6))
    for part in range(per_row):
        normed[zed, part] = (plain[part] / root).astype(BF16)
    r_copies = []
    for step in range(1, n_rot):
        r_copies.append(
            pltpu.make_async_remote_copy(
                src_ref=normed.at[zed],
                dst_ref=normed.at[zed],
                send_sem=r_send.at[step - 1],
                recv_sem=r_recv.at[step - 1],
                device_id=rot_peer(step),
                device_id_type=MESH,
            )
        )
        r_copies[-1].start()

    last = per_row - 1
    turn_references(last)

    def partial(z):
        rows = left[last, pl.ds(pl.multiple_of(z * 128, 128), 128), :]
        return product(last, rows) + earlier[z] if last else product(last, rows)

    steps = [n_rot // 2]
    for step in range(n_rot // 2 - 1, 0, -1):
        steps += [lax.select(zed % 2 == 0, n_rot - step, step)]
        steps += [lax.select(zed % 2 == 0, step, n_rot - step)]
    e_copies = []
    for i, step in enumerate(steps):
        outgoing[i] = partial(lax.rem(zed + step, n_rot)).astype(BF16)
        e_copies.append(
            pltpu.make_async_remote_copy(
                src_ref=outgoing.at[i],
                dst_ref=incoming.at[i],
                send_sem=e_send.at[i],
                recv_sem=e_recv.at[i],
                device_id=rot_peer(step),
                device_id_type=MESH,
            )
        )
        e_copies[-1].start()

    squares = jnp.zeros((classes, 128), F32)
    for part in range(per_row):
        for block in range(BLOCKS):
            x = wide[part, pl.ds(block, classes, stride=8), :]
            squares = squares + x * x
    squares = jnp.broadcast_to(jnp.sum(squares, axis=1, keepdims=True), (classes, 128))
    norm_mine[...] = squares.T[:8]
    n_copies = []
    for step in range(1, n_rot):
        n_copies.append(
            pltpu.make_async_remote_copy(
                src_ref=norm_mine,
                dst_ref=norm_in.at[step - 1],
                send_sem=n_send.at[step - 1],
                recv_sem=n_recv.at[step - 1],
                device_id=rot_peer(step),
                device_id_type=MESH,
            )
        )
        n_copies[-1].start()
    found = partial(zed)

    for copy in r_copies:
        copy.wait_recv()
    for z in range(n_rot):
        for part in range(per_row):
            wide[part, :ROWS] = normed[z, part].astype(F32)
            for block in range(BLOCKS):
                first = (block // 4) * CYCLES * MFREQ + z * half
                first += (block % 4) * lanes + part * 128
                values = wide[part, pl.ds(block, CLS, stride=8), :]
                refs_ref[:, first : first + 128] = values.astype(BF16)

    for copy in n_copies:
        copy.wait_recv()
    spread = norm_mine[...]
    for step in range(n_rot - 1):
        spread = spread + norm_in[step]
    scale = (1.0 / math.sqrt(K)) / jnp.sqrt(spread / K + 1e-6)

    for i, copy in enumerate(e_copies):
        copy.wait_recv()
        found = found + incoming[i].astype(F32)
    best = found[:classes]
    for fine in range(1, FINE):
        best = jnp.maximum(best, found[fine * classes : fine * classes + classes])
    best = best.T
    top = best[:share]
    for a in range(1, coarse):
        top = jnp.maximum(top, best[a * share : a * share + share])
    scores_ref[...] = top * scale[:1]

    for copy in sum(a_copies + c_copies, []) + s_copies + r_copies + e_copies + n_copies:
        copy.wait_send()


def write_out(refs, scores, refs_out, scores_out, sem):
    copies = [
        pltpu.make_async_copy(refs, refs_out, sem.at[0]),
        pltpu.make_async_copy(scores, scores_out, sem.at[1]),
    ]
    for copy in copies:
        copy.start()
    for copy in copies:
        copy.wait()


def trig_table(total):
    freqs = np.arange(128) % MFREQ
    phase = (np.arange(total)[:, None] * freqs[None, :]) % total * (2.0 * math.pi / total)
    return np.concatenate([np.cos(phase), np.sin(phase)], axis=1).astype(np.float32)


def local(n_dom, n_rot, particles, assign, rot_index, group, ctf_table):
    count = particles.shape[0]
    total = 8 * n_rot
    share = count // n_rot
    lanes = CYCLES // n_rot * MFREQ // 4
    half = 4 * lanes
    per_row = lanes // 128
    classes = CLS * n_dom
    vmem = pl.BlockSpec(memory_space=pltpu.VMEM)
    dma = pltpu.SemaphoreType.DMA
    parts, rot = dma((per_row, n_dom - 1)), dma((n_rot - 1,))
    shapes = (
        jax.ShapeDtypeStruct((CLS, K), BF16),
        jax.ShapeDtypeStruct((share, classes), F32),
    )
    results = pl.pallas_call(
        functools.partial(kernel, n_dom, n_rot),
        out_shape=shapes,
        in_specs=[pl.BlockSpec(memory_space=pltpu.HBM)] * 6,
        out_specs=(vmem, vmem),
        scratch_shapes=[
            pltpu.VMEM((2, count, half), BF16),
            pltpu.VMEM((1, count), jnp.int32),
            pltpu.VMEM((1, count), jnp.int32),
            pltpu.VMEM((1, count), jnp.int32),
            pltpu.VMEM(ctf_table.shape, F32),
            pltpu.VMEM((total, 256), F32),
            pltpu.VMEM((per_row, n_dom * (ROWS + 8), 128), F32),
            pltpu.VMEM((n_dom - 1, per_row, ROWS + 8, 128), F32),
            pltpu.VMEM((per_row, n_dom, ROWS, 128), BF16),
            pltpu.VMEM((per_row, n_dom * ROWS, 128), F32),
            pltpu.VMEM((8, 128), F32),
            pltpu.VMEM((n_rot - 1, 8, 128), F32),
            pltpu.VMEM((n_rot, per_row, ROWS, 128), BF16),
            pltpu.VMEM((per_row, n_rot * 128, 1024), BF16),
            pltpu.VMEM((per_row, FINE * classes, 1024), BF16),
            pltpu.VMEM((n_rot, FINE * classes, 128), F32),
            pltpu.VMEM((n_rot - 1, FINE * classes, 128), BF16),
            pltpu.VMEM((n_rot - 1, FINE * classes, 128), BF16),
            pltpu.VMEM((8, classes), F32),
            pltpu.VMEM((n_rot - 1, 8, classes), F32),
            dma((7,)),
            parts, parts, parts, parts, rot, rot, rot, rot, rot, rot, rot, rot,
        ],
        compiler_params=pltpu.CompilerParams(
            collective_id=0, has_side_effects=True, vmem_limit_bytes=48 * 1024 * 1024
        ),
    )(
        *(
            pltpu.with_memory_space_constraint(x, pltpu.HBM)
            for x in (
                particles,
                assign.reshape(1, count),
                rot_index.reshape(1, count),
                group.reshape(1, count),
                ctf_table,
                jnp.asarray(trig_table(total)),
            )
        )
    )
    return pl.pallas_call(
        write_out,
        out_shape=shapes,
        in_specs=[vmem, vmem],
        out_specs=[pl.BlockSpec(memory_space=pltpu.HBM)] * 2,
        scratch_shapes=[dma((2,))],
    )(*results)


def solution(mesh):
    sizes = dict(mesh.shape)
    in_specs = (P("dom", None), P("dom"), P("dom"), P("dom"), P())
    out_specs = (P("dom", None), P(("dom", "rot"), None))
    return jax.shard_map(
        functools.partial(local, sizes["dom"], sizes["rot"]),
        mesh=mesh, in_specs=in_specs, out_specs=out_specs, check_vma=False,
    )
```

time: 27.4 us -> 28.4 us (1.036)
  Pallas kernels: 25.3 us -> 26.3 us
    pallas_call x1 -> x2, Pallas kernels: 25.3 us -> 26.3 us  [the longest x1 24.7 us: local(): pl.pallas_call(functools.partial(kernel, n_dom, n_rot), out_shape=shapes,...]
    unnamed x2 -> x4, local copies, waits for them, and re-layouts: 1.26 us -> 1.23 us
where the time goes in v3:
time: 28.4 us; the launch traced here: 28.2 us
  Pallas kernels  26.3 us (93%)
  local copies, waits for them, and re-layouts  1.23 us (4%)
  between operations  0.65 us (2%)
    pallas_call x1, Pallas kernels, local(): pl.pallas_call(functools.partial(kernel, n_dom, n_rot), out_shape=shapes,...  24.7 us
    pallas_call x1, Pallas kernels, local(): pl.pallas_call(write_out, out_shape=shapes, in_specs=[vmem, vmem], out_sp...  1.58 us
    unnamed x4, local copies, waits for them, and re-layouts  1.23 us

profile of v3, /device:TPU:0, one launch (start us, length us, event | category | flops | bytes accessed | tf_op | source)
XLA Modules:
  0.0 28.2 jit_solution(17786321994340836315)
XLA Ops:
  0.6 24.7 %shard_map.77 = (bf16[6,8192]{1,0:T(8,128)(2,1)S(1)}, f32[16,48]{1,0:T(8,128)S(1)}) custom-call(bf16[64,8192]{1,0:T(8,128)(2,1)} %particles_hbm.1, s32[1,64]{1,0:T(1,128)} %bitcast.3, s32[1,64]{1,0:T(1,128)} %bitcast.4, s32[1,64]{1,0:T(1,128)} %bitcast.5, f32[32,64]{1,0:T(8,128)} %table_hbm.1, f32[32,256]{1,0:T(8,128)} %constant.2.clone.trig_hbm), custom_call_target="tpu_custom_call" | custom-call | tf_op jit(solution)/shard_map/pallas_call | solution.py:403
  25.4 0.0 copy-start
  25.4 0.6 %copy-done = bf16[6,8192]{1,0:T(8,128)(2,1)} copy-done((bf16[6,8192]{1,0:T(8,128)(2,1)}, bf16[6,8192]{1,0:T(8,128)(2,1)S(1)}, u32[]{:S(2)}) %copy-start) | copy-done | bytes 98328
  26.0 0.0 copy-start.1
  26.0 0.6 %copy-done.1 = f32[16,48]{1,0:T(8,128)} copy-done((f32[16,48]{1,0:T(8,128)}, f32[16,48]{1,0:T(8,128)S(1)}, u32[]{:S(2)}) %copy-start.1) | copy-done | bytes 3096
  26.6 1.6 %shard_map.78 = (bf16[6,8192]{1,0:T(8,128)(2,1)}, f32[16,48]{1,0:T(8,128)}) custom-call(bf16[6,8192]{1,0:T(8,128)(2,1)} %copy-done, f32[16,48]{1,0:T(8,128)} %copy-done.1), custom_call_target="tpu_custom_call" | custom-call | tf_op jit(solution)/shard_map/pallas_call | solution.py:448
Async XLA Ops:
  25.4 0.6 %copy-start = (bf16[6,8192]{1,0:T(8,128)(2,1)}, bf16[6,8192]{1,0:T(8,128)(2,1)S(1)}, u32[]{:S(2)}) copy-start(bf16[6,8192]{1,0:T(8,128)(2,1)S(1)} %get-tuple-element.4.refs) | copy-start | bytes 294916
  26.0 0.6 %copy-start.1 = (f32[16,48]{1,0:T(8,128)}, f32[16,48]{1,0:T(8,128)S(1)}, u32[]{:S(2)}) copy-start(f32[16,48]{1,0:T(8,128)S(1)} %get-tuple-element.5.scores) | copy-start | bytes 9220

commit v4 on v3

--- a/solution.py
+++ b/solution.py
@@ -59,9 +59,9 @@
     particles_hbm, assign_hbm, rot_hbm, group_hbm, table_hbm, trig_hbm,
     refs_ref, scores_ref,
     spec, assign_ref, rot_ref, group_ref, table_ref, trig_ref,
-    sums, sums_in, plain_all, wide, spread_mine, spread_in, normed, left, right,
+    sums, other_core, sums_in, plain_all, wide, spread_mine, spread_in, normed, left, right,
     earlier, outgoing, incoming, norm_mine, norm_in,
-    load_sem, a_send, a_recv, c_send, c_recv, s_send, s_recv, r_send, r_recv,
+    load_sem, p_send, p_recv, a_send, a_recv, c_send, c_recv, s_send, s_recv, r_send, r_recv,
     e_send, e_recv, n_send, n_recv,
 ):
     me = lax.axis_index("dom")
@@ -75,6 +75,7 @@
     lanes = half // 4
     per_row = lanes // 128
     classes = CLS * n_dom
+    deep = per_row * 24 + 8
     groups = table_ref.shape[0]
 
     barrier = pltpu.get_barrier_semaphore()
@@ -116,16 +117,13 @@
     member = ones_where((place & (n_dom - 1)) * CLS + place // n_dom == labels)
     denom = dot(member, stacked(rows * rows))
     denom = jnp.concatenate([denom, jnp.zeros((classes, 128 - CYCLES), F32)], axis=1)
+
+    def place_rows(c, r, values):
+        at = pl.ds(r, n_dom, stride=deep)
+        sums[c // 3, at, :] = values[c * n_dom : c * n_dom + n_dom]
+
     for c in range(CLS):
-        at = pl.ds(ROWS + c, n_dom, stride=ROWS + 8)
-        sums[0, at, :] = denom[c * n_dom : c * n_dom + n_dom]
-
-    def message(part, owner):
-        first = pl.multiple_of(owner * (ROWS + 8), 8)
-        return sums.at[part, pl.ds(first, ROWS + 8 if part == 0 else ROWS), :]
-
-    def landing(part, step):
-        return sums_in.at[step - 1, part, pl.ds(0, ROWS + 8 if part == 0 else ROWS), :]
+        place_rows(c, per_row * 24 + c % 3, denom)
 
     def lane_tile(block, part):
         first = block * lanes + part * 128
@@ -133,7 +131,6 @@
 
     loads[5].wait()
     loads[6].wait()
-    a_copies = []
     for part in range(per_row):
         for block in range(4):
             lane = lane_tile(block, part)
@@ -144,28 +141,23 @@
             numer = dot(member, stacked(value))
             for c in range(CLS):
                 for i in range(2):
-                    at = pl.ds(c * 8 + i * 4 + block, n_dom, stride=ROWS + 8)
-                    sums[part, at, :] = numer[
-                        c * n_dom : c * n_dom + n_dom, i * 128 : i * 128 + 128
-                    ]
-        if part == 0:
-            pl.semaphore_wait(barrier, n_dom + n_rot - 2)
-        group_copies = []
-        for step in range(1, n_dom):
-            group_copies.append(
-                pltpu.make_async_remote_copy(
-                    src_ref=message(part, lax.rem(me + step, n_dom)),
-                    dst_ref=landing(part, step),
-                    send_sem=a_send.at[part, step - 1],
-                    recv_sem=a_recv.at[part, step - 1],
-                    device_id=dom_peer(step),
-                    device_id_type=MESH,
-                )
-            )
-            group_copies[-1].start()
-        a_copies.append(group_copies)
-
-    for part in range(per_row):
+                    row = part * 24 + c % 3 * 8 + i * 4 + block
+                    place_rows(c, row, numer[:, i * 128 : i * 128 + 128])
+
+    pl.semaphore_wait(barrier, n_dom + n_rot - 2)
+    core = lax.rem(me, 2)
+    chip = me // 2
+    swap = pltpu.make_async_remote_copy(
+        src_ref=sums.at[1 - core],
+        dst_ref=other_core,
+        send_sem=p_send,
+        recv_sem=p_recv,
+        device_id=(me + 1 - 2 * core, zed),
+        device_id_type=MESH,
+    )
+    swap.start()
+
+    def turn_particles(part):
         for block in range(4):
             lane = lane_tile(block, part)
             re = (spec[0, :, lane].astype(F32) * factors[:, lane]).astype(BF16).astype(F32)
@@ -183,26 +175,68 @@
                         [x[z * share : z * share + share] for x in turned], axis=0
                     ).astype(BF16)
 
+    if per_row > 1:
+        turn_particles(0)
+    swap.wait_recv()
+    sums[core] = sums[core] + other_core[...]
+
+    def message(owner):
+        return sums.at[core, pl.ds(pl.multiple_of(owner * deep, 8), deep), :]
+
+    a_copies = []
+    for step in range(n_dom // 2):
+        for target in range(2) if step else [1 - core]:
+            owner = lax.rem(chip + step, n_dom // 2) * 2 + target
+            a_copies.append(
+                pltpu.make_async_remote_copy(
+                    src_ref=message(owner),
+                    dst_ref=sums_in.at[core, step],
+                    send_sem=a_send.at[len(a_copies)],
+                    recv_sem=a_recv.at[core, step],
+                    device_id=(owner, zed),
+                    device_id_type=MESH,
+                )
+            )
+    for copy in a_copies[1:] + a_copies[:1]:
+        copy.start()
+    sums_in[core, 0] = message(me)[...]
+    for part in range(1 if per_row > 1 else 0, per_row):
+        turn_particles(part)
+
     cb = cyc // 4
     offset = iota((ROWS, 128), 1) - zed * cyc
     low = (iota((ROWS, 128), 0) & 3) * cb
     shape = (3 * 128, lanes)
     spreader = ones_where((iota(shape, 0) & (cb - 1)) == iota(shape, 1) // MFREQ)
 
+    for step in range(n_dom // 2):
+        for source in range(2) if step else [1 - core]:
+            pltpu.make_async_remote_copy(
+                src_ref=sums_in.at[source, step],
+                dst_ref=sums_in.at[source, step],
+                send_sem=p_send,
+                recv_sem=a_recv.at[source, step],
+                device_id=(me + 1 - 2 * core, zed),
+                device_id_type=MESH,
+            ).wait_recv()
+    whole = sums_in[:, 0]
+    for step in range(1, n_dom // 2):
+        whole = whole + sums_in[:, step]
+    denom = jnp.concatenate(
+        [
+            jnp.broadcast_to(whole[c // 3, per_row * 24 + c % 3][None], (8, 128))
+            for c in range(CLS)
+        ],
+        axis=0,
+    )
+    denom = jnp.where((offset >= low) & (offset < low + cb), denom, 0.0)
+    denom = dot(jnp.concatenate(pieces(denom), axis=1), spreader) + 1.0
+
     c_copies = []
     plain = []
     for part in range(per_row):
-        for copy in a_copies[part]:
-            copy.wait_recv()
-        whole = message(part, me)[...]
-        for step in range(1, n_dom):
-            whole = whole + landing(part, step)[...]
-        if part == 0:
-            denom = jnp.where(
-                (offset >= low) & (offset < low + cb), each_row(whole[ROWS:]), 0.0
-            )
-            denom = dot(jnp.concatenate(pieces(denom), axis=1), spreader) + 1.0
-        plain.append(whole[:ROWS] / denom[:, part * 128 : part * 128 + 128])
+        numer = jnp.concatenate([whole[i, part * 24 : part * 24 + 24] for i in range(2)], axis=0)
+        plain.append(numer / denom[:, part * 128 : part * 128 + 128])
         plain_all[part, me] = plain[-1].astype(BF16)
         group_copies = []
         for step in range(1, n_dom):
@@ -364,19 +398,8 @@
         top = jnp.maximum(top, best[a * share : a * share + share])
     scores_ref[...] = top * scale[:1]
 
-    for copy in sum(a_copies + c_copies, []) + s_copies + r_copies + e_copies + n_copies:
+    for copy in [swap] + a_copies + sum(c_copies, []) + s_copies + r_copies + e_copies + n_copies:
         copy.wait_send()
-
-
-def write_out(refs, scores, refs_out, scores_out, sem):
-    copies = [
-        pltpu.make_async_copy(refs, refs_out, sem.at[0]),
-        pltpu.make_async_copy(scores, scores_out, sem.at[1]),
-    ]
-    for copy in copies:
-        copy.start()
-    for copy in copies:
-        copy.wait()
 
 
 def trig_table(total):
@@ -395,12 +418,13 @@
     classes = CLS * n_dom
     vmem = pl.BlockSpec(memory_space=pltpu.VMEM)
     dma = pltpu.SemaphoreType.DMA
+    deep = per_row * 24 + 8
     parts, rot = dma((per_row, n_dom - 1)), dma((n_rot - 1,))
     shapes = (
         jax.ShapeDtypeStruct((CLS, K), BF16),
         jax.ShapeDtypeStruct((share, classes), F32),
     )
-    results = pl.pallas_call(
+    return pl.pallas_call(
         functools.partial(kernel, n_dom, n_rot),
         out_shape=shapes,
         in_specs=[pl.BlockSpec(memory_space=pltpu.HBM)] * 6,
@@ -412,8 +436,9 @@
             pltpu.VMEM((1, count), jnp.int32),
             pltpu.VMEM(ctf_table.shape, F32),
             pltpu.VMEM((total, 256), F32),
-            pltpu.VMEM((per_row, n_dom * (ROWS + 8), 128), F32),
-            pltpu.VMEM((n_dom - 1, per_row, ROWS + 8, 128), F32),
+            pltpu.VMEM((2, n_dom * deep, 128), F32),
+            pltpu.VMEM((n_dom * deep, 128), F32),
+            pltpu.VMEM((2, n_dom // 2, deep, 128), F32),
             pltpu.VMEM((per_row, n_dom, ROWS, 128), BF16),
             pltpu.VMEM((per_row, n_dom * ROWS, 128), F32),
             pltpu.VMEM((8, 128), F32),
@@ -426,8 +451,8 @@
             pltpu.VMEM((n_rot - 1, FINE * classes, 128), BF16),
             pltpu.VMEM((8, classes), F32),
             pltpu.VMEM((n_rot - 1, 8, classes), F32),
-            dma((7,)),
-            parts, parts, parts, parts, rot, rot, rot, rot, rot, rot, rot, rot,
+            dma((7,)), dma(()), dma(()),
+            dma((n_dom - 1,)), dma((2, n_dom // 2)), parts, parts, rot, rot, rot, rot, rot, rot, rot, rot,
         ],
         compiler_params=pltpu.CompilerParams(
             collective_id=0, has_side_effects=True, vmem_limit_bytes=48 * 1024 * 1024
@@ -445,13 +470,6 @@
             )
         )
     )
-    return pl.pallas_call(
-        write_out,
-        out_shape=shapes,
-        in_specs=[vmem, vmem],
-        out_specs=[pl.BlockSpec(memory_space=pltpu.HBM)] * 2,
-        scratch_shapes=[dma((2,))],
-    )(*results)
 
 
 def solution(mesh):

time: 28.4 us -> 27.5 us (0.968)
  Pallas kernels: 26.3 us -> 25.4 us
    pallas_call x1 -> x0, Pallas kernels: 1.58 us -> none  [local(): pl.pallas_call(write_out, out_shape=shapes, in_specs=[vmem, vmem], out_sp...]
    pallas_call x1, Pallas kernels: 24.7 us -> 25.4 us  [local(): pl.pallas_call(functools.partial(kernel, n_dom, n_rot), out_shape=shapes,...]
    unnamed x4 -> x2, local copies, waits for them, and re-layouts: 1.23 us -> 1.26 us
where the time goes in v4:
time: 27.5 us; the launch traced here: 27.3 us
  Pallas kernels  25.4 us (92%)
  local copies, waits for them, and re-layouts  1.26 us (5%)
  between operations  0.64 us (2%)
    pallas_call x1, Pallas kernels, local(): pl.pallas_call(functools.partial(kernel, n_dom, n_rot), out_shape=shapes,...  25.4 us
    unnamed x2, local copies, waits for them, and re-layouts  1.26 us

profile of v4, /device:TPU:0, one launch (start us, length us, event | category | flops | bytes accessed | tf_op | source)
XLA Modules:
  0.0 27.3 jit_solution(11702233834055760160)
XLA Ops:
  0.6 25.4 %shard_map.77 = (bf16[6,8192]{1,0:T(8,128)(2,1)S(1)}, f32[16,48]{1,0:T(8,128)S(1)}) custom-call(bf16[64,8192]{1,0:T(8,128)(2,1)} %particles_hbm.1, s32[1,64]{1,0:T(1,128)} %bitcast.3, s32[1,64]{1,0:T(1,128)} %bitcast.4, s32[1,64]{1,0:T(1,128)} %bitcast.5, f32[32,64]{1,0:T(8,128)} %table_hbm.1, f32[32,256]{1,0:T(8,128)} %constant.2.clone.trig_hbm), custom_call_target="tpu_custom_call" | custom-call | tf_op jit(solution)/shard_map/pallas_call | solution.py:427
  26.1 0.7 %copy.10 = bf16[6,8192]{1,0:T(8,128)(2,1)} copy(bf16[6,8192]{1,0:T(8,128)(2,1)S(1)} %get-tuple-element.4) | data formatting | bytes 196608
  26.7 0.6 %copy.11 = f32[16,48]{1,0:T(8,128)} copy(f32[16,48]{1,0:T(8,128)S(1)} %get-tuple-element.5) | data formatting | bytes 6144

commit v5 on v3

--- a/solution.py
+++ b/solution.py
@@ -368,17 +368,6 @@
         copy.wait_send()
 
 
-def write_out(refs, scores, refs_out, scores_out, sem):
-    copies = [
-        pltpu.make_async_copy(refs, refs_out, sem.at[0]),
-        pltpu.make_async_copy(scores, scores_out, sem.at[1]),
-    ]
-    for copy in copies:
-        copy.start()
-    for copy in copies:
-        copy.wait()
-
-
 def trig_table(total):
     freqs = np.arange(128) % MFREQ
     phase = (np.arange(total)[:, None] * freqs[None, :]) % total * (2.0 * math.pi / total)
@@ -400,7 +389,7 @@
         jax.ShapeDtypeStruct((CLS, K), BF16),
         jax.ShapeDtypeStruct((share, classes), F32),
     )
-    results = pl.pallas_call(
+    return pl.pallas_call(
         functools.partial(kernel, n_dom, n_rot),
         out_shape=shapes,
         in_specs=[pl.BlockSpec(memory_space=pltpu.HBM)] * 6,
@@ -445,13 +434,6 @@
             )
         )
     )
-    return pl.pallas_call(
-        write_out,
-        out_shape=shapes,
-        in_specs=[vmem, vmem],
-        out_specs=[pl.BlockSpec(memory_space=pltpu.HBM)] * 2,
-        scratch_shapes=[dma((2,))],
-    )(*results)
 
 
 def solution(mesh):

time: 28.4 us -> 26.8 us (0.944)
  Pallas kernels: 26.3 us -> 24.7 us
    pallas_call x1 -> x0, Pallas kernels: 1.58 us -> none  [local(): pl.pallas_call(write_out, out_shape=shapes, in_specs=[vmem, vmem], out_sp...]
    unnamed x4 -> x2, local copies, waits for them, and re-layouts: 1.23 us -> 1.26 us
where the time goes in v5:
time: 26.8 us; the launch traced here: 26.6 us
  Pallas kernels  24.7 us (92%)
  local copies, waits for them, and re-layouts  1.26 us (5%)
  between operations  0.64 us (2%)
    pallas_call x1, Pallas kernels, local(): pl.pallas_call(functools.partial(kernel, n_dom, n_rot), out_shape=shapes,...  24.7 us
    unnamed x2, local copies, waits for them, and re-layouts  1.26 us

profile of v5, /device:TPU:0, one launch (start us, length us, event | category | flops | bytes accessed | tf_op | source)
XLA Modules:
  0.0 26.6 jit_solution(14358745973160377868)
XLA Ops:
  0.6 24.7 %shard_map.77 = (bf16[6,8192]{1,0:T(8,128)(2,1)S(1)}, f32[16,48]{1,0:T(8,128)S(1)}) custom-call(bf16[64,8192]{1,0:T(8,128)(2,1)} %particles_hbm.1, s32[1,64]{1,0:T(1,128)} %bitcast.3, s32[1,64]{1,0:T(1,128)} %bitcast.4, s32[1,64]{1,0:T(1,128)} %bitcast.5, f32[32,64]{1,0:T(8,128)} %table_hbm.1, f32[32,256]{1,0:T(8,128)} %constant.2.clone.trig_hbm), custom_call_target="tpu_custom_call" | custom-call | tf_op jit(solution)/shard_map/pallas_call | solution.py:392
  25.4 0.7 %copy.10 = bf16[6,8192]{1,0:T(8,128)(2,1)} copy(bf16[6,8192]{1,0:T(8,128)(2,1)S(1)} %get-tuple-element.4) | data formatting | bytes 196608
  26.0 0.6 %copy.11 = f32[16,48]{1,0:T(8,128)} copy(f32[16,48]{1,0:T(8,128)S(1)} %get-tuple-element.5) | data formatting | bytes 6144

commit v6 on v5

--- a/solution.py
+++ b/solution.py
@@ -60,7 +60,7 @@
     refs_ref, scores_ref,
     spec, assign_ref, rot_ref, group_ref, table_ref, trig_ref,
     sums, sums_in, plain_all, wide, spread_mine, spread_in, normed, left, right,
-    earlier, outgoing, incoming, norm_mine, norm_in,
+    square_rows, outgoing, incoming, norm_mine, norm_in,
     load_sem, a_send, a_recv, c_send, c_recv, s_send, s_recv, r_send, r_recv,
     e_send, e_recv, n_send, n_recv,
 ):
@@ -177,9 +177,9 @@
                 turned_re.append(re * cos + im * sin)
                 turned_im.append(im * cos - re * sin)
             for i, turned in enumerate((turned_re, turned_im)):
-                first = (i * 4 + block) * 128
+                first = part * 1024 + (i * 4 + block) * 128
                 for z in range(n_rot):
-                    left[part, z * 128 : z * 128 + 128, first : first + 128] = jnp.concatenate(
+                    left[z * 128 : z * 128 + 128, first : first + 128] = jnp.concatenate(
                         [x[z * share : z * share + share] for x in turned], axis=0
                     ).astype(BF16)
 
@@ -189,7 +189,6 @@
     shape = (3 * 128, lanes)
     spreader = ones_where((iota(shape, 0) & (cb - 1)) == iota(shape, 1) // MFREQ)
 
-    c_copies = []
     plain = []
     for part in range(per_row):
         for copy in a_copies[part]:
@@ -203,21 +202,27 @@
             )
             denom = dot(jnp.concatenate(pieces(denom), axis=1), spreader) + 1.0
         plain.append(whole[:ROWS] / denom[:, part * 128 : part * 128 + 128])
-        plain_all[part, me] = plain[-1].astype(BF16)
-        group_copies = []
-        for step in range(1, n_dom):
-            group_copies.append(
+        plain_all[me, part] = plain[-1].astype(BF16)
+
+    many = n_dom // 2
+    own_half = me // many
+    halves = [own_half, 1 - own_half]
+    spot = me - own_half * many
+    c_copies = [[], []]
+    for side in range(2):
+        for step in range(1 - side, many):
+            peer = halves[side] * many + lax.rem(spot + step, many)
+            c_copies[side].append(
                 pltpu.make_async_remote_copy(
-                    src_ref=plain_all.at[part, me],
-                    dst_ref=plain_all.at[part, me],
-                    send_sem=c_send.at[part, step - 1],
-                    recv_sem=c_recv.at[part, step - 1],
-                    device_id=dom_peer(step),
+                    src_ref=plain_all.at[me],
+                    dst_ref=plain_all.at[me],
+                    send_sem=c_send.at[side, step],
+                    recv_sem=c_recv.at[side, step],
+                    device_id=(peer, zed),
                     device_id_type=MESH,
                 )
             )
-            group_copies[-1].start()
-        c_copies.append(group_copies)
+            c_copies[side][-1].start()
 
     squares = sum(jnp.sum((x * x).reshape(CLS, 8, 128), axis=1) for x in plain)
     squares = jnp.broadcast_to(jnp.sum(squares, axis=1, keepdims=True), (CLS, 128))
@@ -236,33 +241,61 @@
         )
         s_copies[-1].start()
 
-    def turn_references(part):
-        for copy in c_copies[part]:
+    some = classes // 2
+
+    def turn_references(side):
+        for copy in c_copies[side]:
             copy.wait_recv()
-        wide[part] = plain_all[part].astype(F32).reshape(classes * 8, 128)
-        blocks = [wide[part, pl.ds(block, classes, stride=8), :] for block in range(BLOCKS)]
-        for fine in range(FINE):
-            cos = trig_ref[fine : fine + 1, :128]
-            sin = trig_ref[fine : fine + 1, 128:]
-            at = slice(fine * classes, fine * classes + classes)
-            for block in range(4):
-                re, im = blocks[block], blocks[block + 4]
-                lane = slice(block * 128, block * 128 + 128)
-                right[part, at, lane] = (re * cos - im * sin).astype(BF16)
-                lane = slice(block * 128 + 512, block * 128 + 640)
-                right[part, at, lane] = (re * sin + im * cos).astype(BF16)
-
-    def product(part, rows):
+        squares = jnp.zeros((some, 128), F32)
+        for part in range(per_row):
+            mine = plain_all[pl.ds(halves[side] * many, many), part]
+            wide[side, part] = mine.astype(F32).reshape(some * 8, 128)
+            blocks = [wide[side, part, pl.ds(block, some, stride=8), :] for block in range(BLOCKS)]
+            for block in blocks:
+                squares = squares + block * block
+            for fine in range(FINE):
+                cos = trig_ref[fine : fine + 1, :128]
+                sin = trig_ref[fine : fine + 1, 128:]
+                at = slice(fine * some, fine * some + some)
+                for block in range(4):
+                    re, im = blocks[block], blocks[block + 4]
+                    first = part * 1024 + block * 128
+                    right[side, at, first : first + 128] = (re * cos - im * sin).astype(BF16)
+                    first += 512
+                    right[side, at, first : first + 128] = (re * sin + im * cos).astype(BF16)
+        squares = jnp.broadcast_to(jnp.sum(squares, axis=1, keepdims=True), (some, 128))
+        square_rows[pl.ds(pl.multiple_of(halves[side] * some, 8), some), :] = squares
+
+    def partial(side, z):
         return lax.dot_general(
-            right[part], rows, (((1,), (1,)), ((), ())), preferred_element_type=F32
+            right[side],
+            left[pl.ds(pl.multiple_of(z * 128, 128), 128), :],
+            (((1,), (1,)), ((), ())),
+            preferred_element_type=F32,
         )
 
-    for part in range(per_row - 1):
-        turn_references(part)
-        found = product(part, left[part])
-        for z in range(n_rot):
-            first = found[:, z * 128 : z * 128 + 128]
-            earlier[z] = first if part == 0 else earlier[z] + first
+    steps = [n_rot // 2]
+    for step in range(n_rot // 2 - 1, 0, -1):
+        steps += [lax.select(zed % 2 == 0, n_rot - step, step)]
+        steps += [lax.select(zed % 2 == 0, step, n_rot - step)]
+    e_copies = []
+
+    def send_partials(side):
+        for i, step in enumerate(steps):
+            outgoing[side, i] = partial(side, lax.rem(zed + step, n_rot)).astype(BF16)
+            copy = pltpu.make_async_remote_copy(
+                src_ref=outgoing.at[side, i],
+                dst_ref=incoming.at[side, i],
+                send_sem=e_send.at[side, i],
+                recv_sem=e_recv.at[side, i],
+                device_id=rot_peer(step),
+                device_id_type=MESH,
+            )
+            copy.start()
+            e_copies.append(copy)
+
+    turn_references(0)
+    send_partials(0)
 
     for copy in s_copies:
         copy.wait_recv()
@@ -286,39 +319,10 @@
         )
         r_copies[-1].start()
 
-    last = per_row - 1
-    turn_references(last)
-
-    def partial(z):
-        rows = left[last, pl.ds(pl.multiple_of(z * 128, 128), 128), :]
-        return product(last, rows) + earlier[z] if last else product(last, rows)
-
-    steps = [n_rot // 2]
-    for step in range(n_rot // 2 - 1, 0, -1):
-        steps += [lax.select(zed % 2 == 0, n_rot - step, step)]
-        steps += [lax.select(zed % 2 == 0, step, n_rot - step)]
-    e_copies = []
-    for i, step in enumerate(steps):
-        outgoing[i] = partial(lax.rem(zed + step, n_rot)).astype(BF16)
-        e_copies.append(
-            pltpu.make_async_remote_copy(
-                src_ref=outgoing.at[i],
-                dst_ref=incoming.at[i],
-                send_sem=e_send.at[i],
-                recv_sem=e_recv.at[i],
-                device_id=rot_peer(step),
-                device_id_type=MESH,
-            )
-        )
-        e_copies[-1].start()
-
-    squares = jnp.zeros((classes, 128), F32)
-    for part in range(per_row):
-        for block in range(BLOCKS):
-            x = wide[part, pl.ds(block, classes, stride=8), :]
-            squares = squares + x * x
-    squares = jnp.broadcast_to(jnp.sum(squares, axis=1, keepdims=True), (classes, 128))
-    norm_mine[...] = squares.T[:8]
+    turn_references(1)
+    send_partials(1)
+
+    norm_mine[...] = square_rows[...].T[:8]
     n_copies = []
     for step in range(1, n_rot):
         n_copies.append(
@@ -332,17 +336,17 @@
             )
         )
         n_copies[-1].start()
-    found = partial(zed)
+    found = [partial(side, zed) for side in range(2)]
 
     for copy in r_copies:
         copy.wait_recv()
     for z in range(n_rot):
         for part in range(per_row):
-            wide[part, :ROWS] = normed[z, part].astype(F32)
+            wide[0, part, :ROWS] = normed[z, part].astype(F32)
             for block in range(BLOCKS):
                 first = (block // 4) * CYCLES * MFREQ + z * half
                 first += (block % 4) * lanes + part * 128
-                values = wide[part, pl.ds(block, CLS, stride=8), :]
+                values = wide[0, part, pl.ds(block, CLS, stride=8), :]
                 refs_ref[:, first : first + 128] = values.astype(BF16)
 
     for copy in n_copies:
@@ -352,12 +356,16 @@
         spread = spread + norm_in[step]
     scale = (1.0 / math.sqrt(K)) / jnp.sqrt(spread / K + 1e-6)
 
-    for i, copy in enumerate(e_copies):
-        copy.wait_recv()
-        found = found + incoming[i].astype(F32)
-    best = found[:classes]
-    for fine in range(1, FINE):
-        best = jnp.maximum(best, found[fine * classes : fine * classes + classes])
+    for side in range(2):
+        whole = found[side]
+        for i in range(n_rot - 1):
+            e_copies[side * (n_rot - 1) + i].wait_recv()
+            whole = whole + incoming[side, i].astype(F32)
+        best = whole[:some]
+        for fine in range(1, FINE):
+            best = jnp.maximum(best, whole[fine * some : fine * some + some])
+        square_rows[pl.ds(pl.multiple_of(halves[side] * some, 8), some), :] = best
+    best = square_rows[...]
     best = best.T
     top = best[:share]
     for a in range(1, coarse):
@@ -384,6 +392,7 @@
     classes = CLS * n_dom
     vmem = pl.BlockSpec(memory_space=pltpu.VMEM)
     dma = pltpu.SemaphoreType.DMA
+    sides = dma((2, n_dom // 2))
     parts, rot = dma((per_row, n_dom - 1)), dma((n_rot - 1,))
     shapes = (
         jax.ShapeDtypeStruct((CLS, K), BF16),
@@ -403,20 +412,21 @@
             pltpu.VMEM((total, 256), F32),
             pltpu.VMEM((per_row, n_dom * (ROWS + 8), 128), F32),
             pltpu.VMEM((n_dom - 1, per_row, ROWS + 8, 128), F32),
-            pltpu.VMEM((per_row, n_dom, ROWS, 128), BF16),
-            pltpu.VMEM((per_row, n_dom * ROWS, 128), F32),
+            pltpu.VMEM((n_dom, per_row, ROWS, 128), BF16),
+            pltpu.VMEM((2, per_row, n_dom // 2 * ROWS, 128), F32),
             pltpu.VMEM((8, 128), F32),
             pltpu.VMEM((n_rot - 1, 8, 128), F32),
             pltpu.VMEM((n_rot, per_row, ROWS, 128), BF16),
-            pltpu.VMEM((per_row, n_rot * 128, 1024), BF16),
-            pltpu.VMEM((per_row, FINE * classes, 1024), BF16),
-            pltpu.VMEM((n_rot, FINE * classes, 128), F32),
-            pltpu.VMEM((n_rot - 1, FINE * classes, 128), BF16),
-            pltpu.VMEM((n_rot - 1, FINE * classes, 128), BF16),
+            pltpu.VMEM((n_rot * 128, per_row * 1024), BF16),
+            pltpu.VMEM((2, FINE * classes // 2, per_row * 1024), BF16),
+            pltpu.VMEM((classes, 128), F32),
+            pltpu.VMEM((2, n_rot - 1, FINE * classes // 2, 128), BF16),
+            pltpu.VMEM((2, n_rot - 1, FINE * classes // 2, 128), BF16),
             pltpu.VMEM((8, classes), F32),
             pltpu.VMEM((n_rot - 1, 8, classes), F32),
             dma((7,)),
-            parts, parts, parts, parts, rot, rot, rot, rot, rot, rot, rot, rot,
+            parts, parts, sides, sides, rot, rot, rot, rot,
+            dma((2, n_rot - 1)), dma((2, n_rot - 1)), rot, rot,
         ],
         compiler_params=pltpu.CompilerParams(
             collective_id=0, has_side_effects=True, vmem_limit_bytes=48 * 1024 * 1024

time: 26.8 us -> 28.1 us (1.049)
  Pallas kernels: 24.7 us -> 26.1 us
    pallas_call x1, Pallas kernels: 24.7 us -> 26.1 us  [local(): pl.pallas_call(functools.partial(kernel, n_dom, n_rot), out_shape=shapes,...]
where the time goes in v6:
time: 28.1 us; the launch traced here: 28 us
  Pallas kernels  26.1 us (93%)
  local copies, waits for them, and re-layouts  1.26 us (4%)
  between operations  0.64 us (2%)
    pallas_call x1, Pallas kernels, local(): pl.pallas_call(functools.partial(kernel, n_dom, n_rot), out_shape=shapes,...  26.1 us
    unnamed x2, local copies, waits for them, and re-layouts  1.26 us

profile of v6, /device:TPU:0, one launch (start us, length us, event | category | flops | bytes accessed | tf_op | source)
XLA Modules:
  0.0 28.0 jit_solution(12336401206079295641)
XLA Ops:
  0.6 26.1 %shard_map.77 = (bf16[6,8192]{1,0:T(8,128)(2,1)S(1)}, f32[16,48]{1,0:T(8,128)S(1)}) custom-call(bf16[64,8192]{1,0:T(8,128)(2,1)} %particles_hbm.1, s32[1,64]{1,0:T(1,128)} %bitcast.3, s32[1,64]{1,0:T(1,128)} %bitcast.4, s32[1,64]{1,0:T(1,128)} %bitcast.5, f32[32,64]{1,0:T(8,128)} %table_hbm.1, f32[32,256]{1,0:T(8,128)} %constant.2.clone.trig_hbm), custom_call_target="tpu_custom_call" | custom-call | tf_op jit(solution)/shard_map/pallas_call | solution.py:401
  26.7 0.7 %copy.10 = bf16[6,8192]{1,0:T(8,128)(2,1)} copy(bf16[6,8192]{1,0:T(8,128)(2,1)S(1)} %get-tuple-element.4) | data formatting | bytes 196608
  27.4 0.6 %copy.11 = f32[16,48]{1,0:T(8,128)} copy(f32[16,48]{1,0:T(8,128)S(1)} %get-tuple-element.5) | data formatting | bytes 6144

commit v7 on v5

--- a/solution.py
+++ b/solution.py
@@ -165,23 +165,39 @@
             group_copies[-1].start()
         a_copies.append(group_copies)
 
+    steps = [n_rot // 2]
+    for step in range(n_rot // 2 - 1, 0, -1):
+        steps += [lax.select(zed % 2 == 0, n_rot - step, step)]
+        steps += [lax.select(zed % 2 == 0, step, n_rot - step)]
+    shape = (count, 128)
+    spread_out = jnp.concatenate(
+        [
+            ones_where(
+                iota(shape, 0) == lax.rem(zed + step, n_rot) * share + (iota(shape, 1) & (share - 1))
+            )
+            for step in steps + [0]
+        ],
+        axis=1,
+    )
+    shape = (3 * total, 128)
+    picked = ones_where((iota(shape, 0) & (total - 1)) == iota(shape, 1) // share * FINE)
+    over = (((0,), (0,)), ((), ()))
+    table = stacked(trig_ref[...])
+    cos_down = lax.dot_general(table[:, :128], picked, over, preferred_element_type=F32)
+    sin_down = lax.dot_general(table[:, 128:], picked, over, preferred_element_type=F32)
     for part in range(per_row):
         for block in range(4):
             lane = lane_tile(block, part)
-            re = (spec[0, :, lane].astype(F32) * factors[:, lane]).astype(BF16).astype(F32)
-            im = (spec[1, :, lane].astype(F32) * factors[:, lane]).astype(BF16).astype(F32)
-            turned_re, turned_im = [], []
-            for a in range(coarse):
-                cos = trig_ref[a * FINE : a * FINE + 1, :128]
-                sin = trig_ref[a * FINE : a * FINE + 1, 128:]
-                turned_re.append(re * cos + im * sin)
-                turned_im.append(im * cos - re * sin)
-            for i, turned in enumerate((turned_re, turned_im)):
-                first = (i * 4 + block) * 128
-                for z in range(n_rot):
-                    left[part, z * 128 : z * 128 + 128, first : first + 128] = jnp.concatenate(
-                        [x[z * share : z * share + share] for x in turned], axis=0
-                    ).astype(BF16)
+            re = (spec[0, :, lane].astype(F32) * factors[:, lane]).T.astype(BF16)
+            im = (spec[1, :, lane].astype(F32) * factors[:, lane]).T.astype(BF16)
+            for i in range(n_rot):
+                at = slice(i * 128, i * 128 + 128)
+                real = dot(re, spread_out[:, at])
+                imag = dot(im, spread_out[:, at])
+                first = block * 128
+                left[part, first : first + 128, at] = (real * cos_down + imag * sin_down).astype(BF16)
+                first = block * 128 + 512
+                left[part, first : first + 128, at] = (imag * cos_down - real * sin_down).astype(BF16)
 
     cb = cyc // 4
     offset = iota((ROWS, 128), 1) - zed * cyc
@@ -252,17 +268,10 @@
                 lane = slice(block * 128 + 512, block * 128 + 640)
                 right[part, at, lane] = (re * sin + im * cos).astype(BF16)
 
-    def product(part, rows):
-        return lax.dot_general(
-            right[part], rows, (((1,), (1,)), ((), ())), preferred_element_type=F32
-        )
-
     for part in range(per_row - 1):
         turn_references(part)
-        found = product(part, left[part])
-        for z in range(n_rot):
-            first = found[:, z * 128 : z * 128 + 128]
-            earlier[z] = first if part == 0 else earlier[z] + first
+        found = dot(right[part], left[part])
+        earlier[...] = found if part == 0 else earlier[...] + found
 
     for copy in s_copies:
         copy.wait_recv()
@@ -289,28 +298,26 @@
     last = per_row - 1
     turn_references(last)
 
-    def partial(z):
-        rows = left[last, pl.ds(pl.multiple_of(z * 128, 128), 128), :]
-        return product(last, rows) + earlier[z] if last else product(last, rows)
-
-    steps = [n_rot // 2]
-    for step in range(n_rot // 2 - 1, 0, -1):
-        steps += [lax.select(zed % 2 == 0, n_rot - step, step)]
-        steps += [lax.select(zed % 2 == 0, step, n_rot - step)]
     e_copies = []
-    for i, step in enumerate(steps):
-        outgoing[i] = partial(lax.rem(zed + step, n_rot)).astype(BF16)
-        e_copies.append(
-            pltpu.make_async_remote_copy(
-                src_ref=outgoing.at[i],
-                dst_ref=incoming.at[i],
-                send_sem=e_send.at[i],
-                recv_sem=e_recv.at[i],
-                device_id=rot_peer(step),
-                device_id_type=MESH,
-            )
-        )
-        e_copies[-1].start()
+    for pair in range(n_rot // 2):
+        at = slice(pair * 256, pair * 256 + 256)
+        found = dot(right[last], left[last, :, at])
+        if last:
+            found = found + earlier[:, at]
+        for i in range(2 * pair, min(2 * pair + 2, n_rot - 1)):
+            outgoing[i] = found[:, (i % 2) * 128 : (i % 2) * 128 + 128].astype(BF16)
+            e_copies.append(
+                pltpu.make_async_remote_copy(
+                    src_ref=outgoing.at[i],
+                    dst_ref=incoming.at[i],
+                    send_sem=e_send.at[i],
+                    recv_sem=e_recv.at[i],
+                    device_id=rot_peer(steps[i]),
+                    device_id_type=MESH,
+                )
+            )
+            e_copies[-1].start()
+    found = found[:, 128:]
 
     squares = jnp.zeros((classes, 128), F32)
     for part in range(per_row):
@@ -332,7 +339,6 @@
             )
         )
         n_copies[-1].start()
-    found = partial(zed)
 
     for copy in r_copies:
         copy.wait_recv()
@@ -408,9 +414,9 @@
             pltpu.VMEM((8, 128), F32),
             pltpu.VMEM((n_rot - 1, 8, 128), F32),
             pltpu.VMEM((n_rot, per_row, ROWS, 128), BF16),
-            pltpu.VMEM((per_row, n_rot * 128, 1024), BF16),
+            pltpu.VMEM((per_row, 1024, n_rot * 128), BF16),
             pltpu.VMEM((per_row, FINE * classes, 1024), BF16),
-            pltpu.VMEM((n_rot, FINE * classes, 128), F32),
+            pltpu.VMEM((FINE * classes, n_rot * 128), F32),
             pltpu.VMEM((n_rot - 1, FINE * classes, 128), BF16),
             pltpu.VMEM((n_rot - 1, FINE * classes, 128), BF16),
             pltpu.VMEM((8, classes), F32),

time: 26.8 us -> 26.6 us (level)
  no operation moved by 1% of the time
where the time goes in v7:
time: 26.6 us; the launch traced here: 26.5 us
  Pallas kernels  24.6 us (92%)
  local copies, waits for them, and re-layouts  1.26 us (5%)
  between operations  0.64 us (2%)
    pallas_call x1, Pallas kernels, local(): pl.pallas_call(functools.partial(kernel, n_dom, n_rot), out_shape=shapes,...  24.6 us
    unnamed x2, local copies, waits for them, and re-layouts  1.26 us

profile of v7, /device:TPU:0, one launch (start us, length us, event | category | flops | bytes accessed | tf_op | source)
XLA Modules:
  0.0 26.5 jit_solution(14623935844295536046)
XLA Ops:
  0.6 24.6 %shard_map.77 = (bf16[6,8192]{1,0:T(8,128)(2,1)S(1)}, f32[16,48]{1,0:T(8,128)S(1)}) custom-call(bf16[64,8192]{1,0:T(8,128)(2,1)} %particles_hbm.1, s32[1,64]{1,0:T(1,128)} %bitcast.3, s32[1,64]{1,0:T(1,128)} %bitcast.4, s32[1,64]{1,0:T(1,128)} %bitcast.5, f32[32,64]{1,0:T(8,128)} %table_hbm.1, f32[32,256]{1,0:T(8,128)} %constant.2.clone.trig_hbm), custom_call_target="tpu_custom_call" | custom-call | tf_op jit(solution)/shard_map/pallas_call | solution.py:398
  25.2 0.7 %copy.10 = bf16[6,8192]{1,0:T(8,128)(2,1)} copy(bf16[6,8192]{1,0:T(8,128)(2,1)S(1)} %get-tuple-element.4) | data formatting | bytes 196608
  25.9 0.6 %copy.11 = f32[16,48]{1,0:T(8,128)} copy(f32[16,48]{1,0:T(8,128)S(1)} %get-tuple-element.5) | data formatting | bytes 6144

commit v8 on v7

--- a/solution.py
+++ b/solution.py
@@ -85,11 +85,6 @@
     def rot_peer(step):
         return (me, lax.rem(zed + step, n_rot))
 
-    for step in range(1, n_dom):
-        pl.semaphore_signal(barrier, inc=1, device_id=dom_peer(step), device_id_type=MESH)
-    for step in range(1, n_rot):
-        pl.semaphore_signal(barrier, inc=1, device_id=rot_peer(step), device_id_type=MESH)
-
     pairs = [(group_hbm, group_ref), (table_hbm, table_ref), (rot_hbm, rot_ref)]
     pairs += [(trig_hbm, trig_ref), (assign_hbm, assign_ref)]
     for part in range(2):
@@ -98,6 +93,11 @@
     loads = [pltpu.make_async_copy(x, y, load_sem.at[i]) for i, (x, y) in enumerate(pairs)]
     for load in loads:
         load.start()
+
+    for step in range(1, n_dom):
+        pl.semaphore_signal(barrier, inc=1, device_id=dom_peer(step), device_id_type=MESH)
+    for step in range(1, n_rot):
+        pl.semaphore_signal(barrier, inc=1, device_id=rot_peer(step), device_id_type=MESH)
 
     shape = (3 * CYCLES, half)
     spreader = ones_where((iota(shape, 0) & (CYCLES - 1)) == zed * cyc + iota(shape, 1) // MFREQ)

time: 26.6 us -> 26.6 us (level)
  no operation moved by 1% of the time
where the time goes in v8:
time: 26.6 us; the launch traced here: 26.5 us
  Pallas kernels  24.6 us (92%)
  local copies, waits for them, and re-layouts  1.26 us (5%)
  between operations  0.64 us (2%)
    pallas_call x1, Pallas kernels, local(): pl.pallas_call(functools.partial(kernel, n_dom, n_rot), out_shape=shapes,...  24.6 us
    unnamed x2, local copies, waits for them, and re-layouts  1.26 us

profile of v8, /device:TPU:0, one launch (start us, length us, event | category | flops | bytes accessed | tf_op | source)
XLA Modules:
  0.0 26.5 jit_solution(14389674883423506605)
XLA Ops:
  0.6 24.6 %shard_map.77 = (bf16[6,8192]{1,0:T(8,128)(2,1)S(1)}, f32[16,48]{1,0:T(8,128)S(1)}) custom-call(bf16[64,8192]{1,0:T(8,128)(2,1)} %particles_hbm.1, s32[1,64]{1,0:T(1,128)} %bitcast.3, s32[1,64]{1,0:T(1,128)} %bitcast.4, s32[1,64]{1,0:T(1,128)} %bitcast.5, f32[32,64]{1,0:T(8,128)} %table_hbm.1, f32[32,256]{1,0:T(8,128)} %constant.2.clone.trig_hbm), custom_call_target="tpu_custom_call" | custom-call | tf_op jit(solution)/shard_map/pallas_call | solution.py:398
  25.2 0.7 %copy.10 = bf16[6,8192]{1,0:T(8,128)(2,1)} copy(bf16[6,8192]{1,0:T(8,128)(2,1)S(1)} %get-tuple-element.4) | data formatting | bytes 196608
  25.9 0.6 %copy.11 = f32[16,48]{1,0:T(8,128)} copy(f32[16,48]{1,0:T(8,128)S(1)} %get-tuple-element.5) | data formatting | bytes 6144
